TPU v7x, 256 devices: a whole 4x4x8 slice. The times are simulated.
256 devices in a mesh: seq: 64 (over x, z, core), tp: 4 (over y).
Axes of the slice: x: 4, y: 4, z: 8, core: 2. Of those that a mesh axis runs over, the one named last changes fastest.
Arguments:
- picked: int32 [4096], P('seq'), may hold values from -1 to 16383, as said below
- owner_perm: int32 [64], replicated, may hold values from 0 to 63, each once
- router_logit: bfloat16 [16384], P('seq'), may hold values from -6 to 6
- queries: bfloat16 [4096, 3072], P('seq', 'tp'), may hold values from -6.5 to 6.5
- keys: bfloat16 [4096, 3072], P('seq', 'tp'), may hold values from -6.5 to 6.5
- values: bfloat16 [4096, 3072], P('seq', 'tp'), may hold values from -6 to 6
- out_grad: bfloat16 [2048, 3072], P('seq', 'tp'), may hold values from -6 to 6
Outputs:
- gated_out: bfloat16 [2048, 3072], P('seq', 'tp')
- query_grad: bfloat16 [4096, 3072], P('seq', 'tp')
- key_grad: bfloat16 [4096, 3072], P('seq', 'tp')
- value_grad: bfloat16 [4096, 3072], P('seq', 'tp')
- router_grad: float32 [16384], P('seq')
Inputs may be any that keep to these rules, and one draw needn't show every extreme that they name: Block h lists, in increasing order, the picked positions of shard h (from h * 256 to (h + 1) * 256 - 1), then -1 in its unused entries. All blocks together list exactly 2048 positions, and some block is full.
All inputs are finite; a program needn't handle non-finite values.
Results may differ from a plain program's by a relative error of at most 0.04.
Values may be sent and summed in bfloat16 or wider, within the bound.
A program may use at most 128 MiB of HBM per device.

v0:
```python
import jax
import jax.numpy as jnp
from jax import lax
from jax.sharding import PartitionSpec as P

HEADS = 24
HD = 128


NEG_FILL = -1e30


def split_heads(row_block, head_count):
    return row_block.reshape(row_block.shape[0], head_count, row_block.shape[1] // head_count)


def flat_rows(received):
    return received.reshape((-1,) + received.shape[2:])


def pick_rows(source, row_index, keep_mask):
    gathered_rows = source[row_index]
    shaped = keep_mask.reshape(keep_mask.shape + (1,) * (gathered_rows.ndim - keep_mask.ndim))
    return jnp.where(shaped, gathered_rows, jnp.zeros((), source.dtype))


def attend_rows(
    query_rows,
    query_order,
    query_live,
    key_rows,
    value_rows,
    key_order,
    key_live,
    head_count,
    scale_factor,
):
    allowed = (key_order[None, :] <= query_order[:, None]) & key_live[None, :] & query_live[:, None]
    scores = (
        jnp.einsum(
            "qhd,khd->hqk",
            split_heads(query_rows, head_count),
            split_heads(key_rows, head_count),
            preferred_element_type=jnp.float32,
        )
        * scale_factor
    )
    masked = jnp.where(allowed[None], scores, NEG_FILL)
    row_top = jnp.max(masked, axis=2)
    log_total = row_top + jnp.log(jnp.sum(jnp.exp(masked - row_top[:, :, None]), axis=2))
    weights = jnp.where(allowed[None], jnp.exp(masked - log_total[:, :, None]), 0.0)
    attended = jnp.einsum(
        "hqk,khd->qhd",
        weights.astype(jnp.bfloat16),
        split_heads(value_rows, head_count),
        preferred_element_type=jnp.float32,
    )
    return (attended.reshape(query_rows.shape[0], query_rows.shape[1]), log_total, weights)


def query_side(out_rounded, attended, weights, key_rows, value_rows, head_count, scale_factor):
    grad_heads = split_heads(out_rounded, head_count)
    row_delta = jnp.sum(grad_heads.astype(jnp.float32) * split_heads(attended, head_count), axis=2)
    prob_grad = jnp.einsum(
        "qhd,khd->hqk",
        grad_heads,
        split_heads(value_rows, head_count),
        preferred_element_type=jnp.float32,
    )
    score_grad = (weights * (prob_grad - row_delta.T[:, :, None])).astype(jnp.bfloat16)
    query_grad = (
        jnp.einsum(
            "hqk,khd->qhd",
            score_grad,
            split_heads(key_rows, head_count),
            preferred_element_type=jnp.float32,
        )
        * scale_factor
    )
    return (query_grad.reshape(out_rounded.shape), row_delta)


def key_side(
    key_rows,
    value_rows,
    key_order,
    key_live,
    query_every,
    grad_every,
    total_every,
    delta_every,
    query_order,
    query_live,
    head_count,
    scale_factor,
):
    allowed = (key_order[:, None] <= query_order[None, :]) & key_live[:, None] & query_live[None, :]
    query_heads = split_heads(query_every, head_count)
    grad_heads = split_heads(grad_every, head_count)
    scores = (
        jnp.einsum(
            "khd,qhd->hkq",
            split_heads(key_rows, head_count),
            query_heads,
            preferred_element_type=jnp.float32,
        )
        * scale_factor
    )
    masked = jnp.where(allowed[None], scores, NEG_FILL)
    weights = jnp.where(allowed[None], jnp.exp(masked - total_every.T[:, None, :]), 0.0)
    value_grad = jnp.einsum(
        "hkq,qhd->khd", weights.astype(jnp.bfloat16), grad_heads, preferred_element_type=jnp.float32
    )
    prob_grad = jnp.einsum(
        "khd,qhd->hkq",
        split_heads(value_rows, head_count),
        grad_heads,
        preferred_element_type=jnp.float32,
    )
    score_grad = (weights * (prob_grad - delta_every.T[:, None, :])).astype(jnp.bfloat16)
    key_grad = (
        jnp.einsum("hkq,qhd->khd", score_grad, query_heads, preferred_element_type=jnp.float32)
        * scale_factor
    )
    return (key_grad.reshape(key_rows.shape), value_grad.reshape(value_rows.shape))


def gate_sum(grad_rows, attended):
    partial_sum = jnp.sum(grad_rows.astype(jnp.float32) * attended, axis=1)
    return lax.psum(partial_sum, "tp")


def body(picked, owner_perm, router_logit, queries, keys, values, out_grad):
    seq_size = lax.axis_size("seq")
    capacity = picked.shape[0]
    picks_each = out_grad.shape[0]
    per_peer = capacity // seq_size
    head_count = HEADS // lax.axis_size("tp")
    scale_factor = HD ** (-0.5)
    tokens_here = router_logit.shape[0]
    my_rank = lax.axis_index("seq")
    count_mine = jnp.sum((picked >= 0).astype(jnp.int32))
    all_counts = lax.all_gather(count_mine.reshape(1), "seq", axis=0, tiled=True)
    ends_at = jnp.cumsum(all_counts)
    starts_at = ends_at - all_counts
    start_mine = starts_at[my_rank]
    seq_ranks = jnp.arange(seq_size, dtype=jnp.int32)
    residue = jnp.sum(
        seq_ranks[None, :] * (owner_perm[None, :] == seq_ranks[:, None]).astype(jnp.int32), axis=1
    )
    residue_mine = residue[my_rank]
    slot_ids = jnp.arange(capacity, dtype=jnp.int32)
    home_order = start_mine + slot_ids
    home_live = slot_ids < count_mine
    local_spot = jnp.clip(picked - my_rank * tokens_here, 0, tokens_here - 1)
    home_logit = router_logit[local_spot]
    own_order = jnp.arange(picks_each, dtype=jnp.int32) * seq_size + residue_mine
    peer_slots = jnp.arange(per_peer, dtype=jnp.int32)
    rows_sent = peer_slots[None, :] * seq_size + ((residue - start_mine) % seq_size)[:, None]
    sent_keep = rows_sent < count_mine
    rows_clipped = jnp.minimum(rows_sent, capacity - 1)
    owner_home = jnp.sum((ends_at[None, :] <= own_order[:, None]).astype(jnp.int32), axis=1)
    from_homes = owner_home * per_peer + (own_order - starts_at[owner_home]) // seq_size
    rows_wanted = peer_slots[None, :] * seq_size + ((residue_mine - starts_at) % seq_size)[:, None]
    back_keep = rows_wanted < all_counts[:, None]
    spot_back = jnp.minimum((starts_at[:, None] + rows_wanted) // seq_size, picks_each - 1)
    from_owners = owner_perm[home_order % seq_size] * per_peer + slot_ids // seq_size
    key_all, value_all = (
        lax.all_gather(keys, "seq", axis=0, tiled=True),
        lax.all_gather(values, "seq", axis=0, tiled=True),
    )
    key_order = (starts_at[:, None] + slot_ids[None, :]).reshape(-1)
    key_live = (slot_ids[None, :] < all_counts[:, None]).reshape(-1)
    attended, log_total, weights = attend_rows(
        queries,
        home_order,
        home_live,
        key_all,
        value_all,
        key_order,
        key_live,
        head_count,
        scale_factor,
    )
    gate_value = jax.nn.sigmoid(home_logit.astype(jnp.float32))
    gated = (gate_value[:, None] * attended).astype(jnp.bfloat16)
    arrived = lax.all_to_all(
        pick_rows(gated, rows_clipped, sent_keep), "seq", split_axis=0, concat_axis=0, tiled=True
    )
    gated_out = flat_rows(arrived)[from_homes]
    returned = lax.all_to_all(
        pick_rows(out_grad, spot_back, back_keep), "seq", split_axis=0, concat_axis=0, tiled=True
    )
    grad_rows = pick_rows(flat_rows(returned), from_owners, home_live)
    gate_grad = gate_sum(grad_rows, attended)
    logit_grad = jnp.where(home_live, gate_grad * gate_value * (1.0 - gate_value), 0.0)
    out_rounded = (gate_value[:, None] * grad_rows.astype(jnp.float32)).astype(jnp.bfloat16)
    query_grad, row_delta = query_side(
        out_rounded, attended, weights, key_all, value_all, head_count, scale_factor
    )
    query_every, grad_every = (
        lax.all_gather(queries, "seq", axis=0, tiled=True),
        lax.all_gather(out_rounded, "seq", axis=0, tiled=True),
    )
    total_every, delta_every = (
        lax.all_gather(log_total.T, "seq", axis=0, tiled=True),
        lax.all_gather(row_delta, "seq", axis=0, tiled=True),
    )
    key_grad, value_grad = key_side(
        keys,
        values,
        home_order,
        home_live,
        query_every,
        grad_every,
        total_every,
        delta_every,
        key_order,
        key_live,
        head_count,
        scale_factor,
    )
    live_rows = home_live[:, None]
    query_grad = jnp.where(live_rows, query_grad, 0.0).astype(jnp.bfloat16)
    key_grad = jnp.where(live_rows, key_grad, 0.0).astype(jnp.bfloat16)
    value_grad = jnp.where(live_rows, value_grad, 0.0).astype(jnp.bfloat16)
    spot_hits = (
        picked[:, None] - my_rank * tokens_here == jnp.arange(tokens_here, dtype=jnp.int32)[None, :]
    )
    router_grad = jnp.sum(jnp.where(spot_hits, logit_grad[:, None], 0.0), axis=0)
    return (gated_out, query_grad, key_grad, value_grad, router_grad)


def solution(mesh):
    return jax.shard_map(
        body,
        mesh=mesh,
        in_specs=(
            P("seq"),
            P(),
            P("seq"),
            P("seq", "tp"),
            P("seq", "tp"),
            P("seq", "tp"),
            P("seq", "tp"),
        ),
        out_specs=(P("seq", "tp"), P("seq", "tp"), P("seq", "tp"), P("seq", "tp"), P("seq")),
        check_vma=False,
    )
```

profile of v0, /device:TPU:1, one launch (start us, length us, event | category | flops | bytes accessed | tf_op | source)
XLA Modules:
  0.0 374.5 jit_solution(9321945578427515676)
XLA Ops:
  9.4 1.3 dynamic-slice
  10.7 1.3 compare_select_fusion.6
  12.0 1.4 dynamic-update-slice
  13.4 20.8 %all-reduce = s32[64]{0:T(128)S(1)} all-reduce(s32[64]{0:T(128)S(1)} %dynamic-update-slice), channel_id=1, replica_groups=mesh['seq'=64,'tp'=4] {'seq'}, use_global_device_ids=true, to_apply=%add | all-reduce | flops 64 | bytes 512
  34.5 0.8 select_reduce_fusion.1
  36.6 0.7 gather_fusion.4
  39.2 8.5 %all-to-all-start.1 = ((bf16[64,2,384]{2,1,0:T(2,128)(2,1)}), bf16[64,2,384]{2,1,0:T(2,128)(2,1)S(1)}, u32[]{:S(2)}, u32[]{:S(2)}) async-start(bf16[64,2,384]{2,1,0:T(2,128)(2,1)} %reshape.690), calls=%async_computation.1 | async-start | bytes 196608 | tf_op jit(solution)/shard_map/all_to_all | solution.py:191
  49.3 1.4 gather_fusion.5
  50.8 1.4 gather_fusion
  54.0 4.0 %all-to-all-done.1 = bf16[64,2,384]{2,1,0:T(2,128)(2,1)S(1)} async-done(((bf16[64,2,384]{2,1,0:T(2,128)(2,1)}), bf16[64,2,384]{2,1,0:T(2,128)(2,1)S(1)}, u32[]{:S(2)}, u32[]{:S(2)}) %all-to-all-start.1) | async-done | bytes 98336 | tf_op jit(solution)/shard_map/all_to_all | solution.py:191
  58.9 37.2 %all-gather.7.cloned.1.call-done = bf16[4096,768]{1,0:T(8,128)(2,1)} async-done(((bf16[64,768]{1,0:T(8,128)(2,1)}), bf16[4096,768]{1,0:T(8,128)(2,1)}) %all-gather.7.cloned.1.call-update) | async-done | bytes 6291472 | tf_op jit(solution)/shard_map/all_gather | solution.py:169
  96.1 8.8 %copy.85 = bf16[4096,768]{0,1:T(8,128)(2,1)} copy(bf16[4096,768]{1,0:T(8,128)(2,1)} %all-gather.7.cloned.1.call-done) | data formatting | bytes 12582912 | tf_op jit(solution)/shard_map/all_gather | solution.py:169
  104.9 71.7 %all-gather.9.cloned.1.call-done = bf16[4096,768]{1,0:T(8,128)(2,1)} async-done(((bf16[64,768]{1,0:T(8,128)(2,1)}), bf16[4096,768]{1,0:T(8,128)(2,1)}) %all-gather.9.cloned.1.call-update) | async-done | bytes 6291472 | tf_op jit(solution)/shard_map/all_gather | solution.py:170
  176.6 8.8 %copy.88 = bf16[4096,768]{0,1:T(8,128)(2,1)} copy(bf16[4096,768]{1,0:T(8,128)(2,1)} %all-gather.9.cloned.1.call-done) | data formatting | bytes 12582912 | tf_op jit(solution)/shard_map/all_gather | solution.py:170
  185.4 5.0 %fusion.51 = (f32[6,64]{1,0:T(8,128)S(1)}, f32[6,64,4096]{2,1,0:T(8,128)S(1)}) fusion(bf16[4096,6,128]{0,2,1:T(8,128)(2,1)} %bitcast.146, pred[64,4096]{1,0:T(8,128)(4,1)S(1)} %get-tuple-element.13, bf16[64,768]{1,0:T(8,128)(2,1)S(1)} %copy-done.3), kind=kOutput, calls=%fused_computation.127 | convolution fusion | flops 407371392 | bytes 12944896 | tf_op jit(solution)/shard_map/qhd,khd->hqk/dot_general | solution.py:40
  190.4 1.0 exponential_reduce_fusion
  191.4 2.5 fusion.19
  193.9 0.7 multiply_convert_fusion.1
  197.6 1.3 fusion.37
  198.9 42.6 %all-gather = f32[64,64,6]{1,2,0:T(8,128)S(1)} all-gather(f32[1,64,6]{1,2,0:T(8,128)S(1)} %bitcast.160), channel_id=1, replica_groups=mesh['seq'=64,'tp'=4] {'seq'}, dimensions={0}, use_global_device_ids=true | all-gather | bytes 99840 | tf_op jit(solution)/shard_map/all_gather | solution.py:206
  243.8 6.4 %all-to-all-start = ((bf16[64,2,384]{2,1,0:T(2,128)(2,1)}), bf16[64,2,384]{2,1,0:T(2,128)(2,1)S(1)}, u32[]{:S(2)}, u32[]{:S(2)}) async-start(bf16[64,2,384]{2,1,0:T(2,128)(2,1)} %reshape.688), calls=%async_computation | async-start | bytes 196608 | tf_op jit(solution)/shard_map/all_to_all | solution.py:187
  250.2 7.4 %all-gather.11.cloned.1.call-done = bf16[4096,768]{1,0:T(8,128)(2,1)} async-done(((bf16[64,768]{1,0:T(8,128)(2,1)}), bf16[4096,768]{1,0:T(8,128)(2,1)}) %all-gather.11.cloned.1.call-update) | async-done | bytes 6291472 | tf_op jit(solution)/shard_map/all_gather | solution.py:202
  257.6 8.7 %copy.97 = bf16[4096,768]{0,1:T(8,128)(2,1)} copy(bf16[4096,768]{1,0:T(8,128)(2,1)} %all-gather.11.cloned.1.call-done) | data formatting | bytes 12582912 | tf_op jit(solution)/shard_map/all_gather | solution.py:202
  266.3 8.8 %psum.7 = f32[64]{0:T(128)S(1)} all-reduce(f32[64]{0:T(128)S(1)} %get-tuple-element.5), channel_id=1, replica_groups=mesh['seq'=64,'tp'=4] {'tp'}, use_global_device_ids=true, to_apply=%region_8.9 | all-reduce | flops 64 | bytes 512 | tf_op jit(solution)/shard_map/psum | solution.py:130
  275.1 8.1 %exponential_select_fusion = f32[6,64,4096]{2,1,0:T(8,128)} fusion(bf16[4096,6,128]{0,2,1:T(8,128)(2,1)} %bitcast.154, f32[6,4096]{1,0:T(8,128)S(1)} %bitcast.159, pred[64,4096]{1,0:T(8,128)(4,1)S(1)} %get-tuple-element.12, bf16[64,768]{1,0:T(8,128)(2,1)S(1)} %copy-done.5), kind=kOutput, calls=%fused_computation.9 | convolution fusion | flops 408944640 | bytes 13041664 | tf_op jit(solution)/shard_map/khd,qhd->hkq/dot_general | solution.py:101
  283.2 10.8 %fusion.17 = bf16[6,8,8,128]{3,2,1,0:T(8,128)(2,1)S(1)} fusion(bf16[4096,6,128]{0,2,1:T(8,128)(2,1)} %bitcast.147, bf16[4096,6,128]{0,2,1:T(8,128)(2,1)} %bitcast.150, f32[6,64,4096]{2,1,0:T(8,128)} %copy-done.2, f32[6,64]{1,0:T(8,128)S(1)} %bitcast.161, f32[6,64]{1,0:T(8,128)S(1)} %log_add_fusion, pred[64,4096]{1,0:T(8,128)(4,1)S(1)} %get-tuple-element.13, ...), kind=kOutput, calls=%fused_computation.27 | convolution fusion | flops 813465600 | bytes 19336512 | tf_op jit(solution)/shard_map/hqk,khd->qhd/dot_general | solution.py:72
  294.7 44.8 %all-gather.1 = f32[64,64,6]{1,2,0:T(8,128)S(1)} all-gather(f32[1,64,6]{1,2,0:T(8,128)S(1)} %bitcast.162), channel_id=1, replica_groups=mesh['seq'=64,'tp'=4] {'seq'}, dimensions={0}, use_global_device_ids=true | all-gather | bytes 99840 | tf_op jit(solution)/shard_map/all_gather | solution.py:207
  340.5 1.2 gather_fusion.3
  341.7 8.8 %copy.101 = bf16[4096,768]{0,1:T(8,128)(2,1)} copy(bf16[4096,768]{1,0:T(8,128)(2,1)} %all-gather.13.cloned.1.call-done) | data formatting | bytes 12582912 | tf_op jit(solution)/shard_map/all_gather | solution.py:203
  350.5 6.9 %fusion.13 = bf16[6,8,8,128]{3,2,1,0:T(8,128)(2,1)S(1)} fusion(bf16[4096,6,128]{0,2,1:T(8,128)(2,1)} %bitcast.148, f32[6,64,4096]{2,1,0:T(8,128)} %exponential_select_fusion), kind=kOutput, calls=%fused_computation.25 | convolution fusion | flops 404226048 | bytes 12681216 | tf_op jit(solution)/shard_map/hkq,qhd->khd/dot_general | solution.py:111
  357.4 9.7 %fusion.12 = bf16[6,8,8,128]{3,2,1,0:T(8,128)(2,1)S(1)} fusion(bf16[4096,6,128]{0,2,1:T(8,128)(2,1)} %bitcast.155, f32[6,64,4096]{2,1,0:T(8,128)} %exponential_select_fusion, bf16[4096,6,128]{0,2,1:T(8,128)(2,1)} %bitcast.149, f32[6,4096]{1,0:T(8,128)S(1)} %bitcast.158, bf16[64,768]{1,0:T(8,128)(2,1)S(1)} %copy-done.4), kind=kOutput, calls=%fused_computation.24 | convolution fusion | flops 810123264 | bytes 19169280 | tf_op jit(solution)/shard_map/hkq,qhd->khd/dot_general | solution.py:122
  367.2 0.8 fusion.20
  (78 shorter events, 16.7 us)
Async XLA Ops:
  7.2 29.4 %copy-start = (bf16[32,768]{1,0:T(8,128)(2,1)S(1)}, bf16[32,768]{1,0:T(8,128)(2,1)}, u32[]{:S(2)}) copy-start(bf16[32,768]{1,0:T(8,128)(2,1)} %param.13) | copy-start | bytes 147460
  7.2 88.9 %all-gather.7.cloned.1.call-start = ((), (), s32[]{:S(2)}) async-start(), calls=%async_computation.2 | async-start | bytes 6389760 | tf_op jit(solution)/shard_map/all_gather | solution.py:169
  7.9 168.6 %all-gather.9.cloned.1.call-start = ((), (), s32[]{:S(2)}) async-start(), calls=%async_computation.3 | async-start | bytes 6389760 | tf_op jit(solution)/shard_map/all_gather | solution.py:170
  8.7 248.9 %all-gather.11.cloned.1.call-start = ((), (), s32[]{:S(2)}) async-start(), calls=%async_computation.4 | async-start | bytes 6389760 | tf_op jit(solution)/shard_map/all_gather | solution.py:202
  39.2 18.9 %all-to-all-start.1 = ((bf16[64,2,384]{2,1,0:T(2,128)(2,1)}), bf16[64,2,384]{2,1,0:T(2,128)(2,1)S(1)}, u32[]{:S(2)}, u32[]{:S(2)}) async-start(bf16[64,2,384]{2,1,0:T(2,128)(2,1)} %reshape.690), calls=%async_computation.1 | async-start | bytes 196608 | tf_op jit(solution)/shard_map/all_to_all | solution.py:191
  47.7 294.1 %all-gather.13.cloned.1.call-start = ((), (), s32[]{:S(2)}) async-start(), calls=%async_computation.5 | async-start | bytes 6389760 | tf_op jit(solution)/shard_map/all_gather | solution.py:203
  104.9 80.5 %copy-start.3 = (bf16[64,768]{1,0:T(8,128)(2,1)S(1)}, bf16[64,768]{1,0:T(8,128)(2,1)}, u32[]{:S(2)}) copy-start(bf16[64,768]{1,0:T(8,128)(2,1)} %param.10) | copy-start | bytes 294916
  185.3 6.0 %slice-start = ((s8[6291456]{0:T(1024)(128)(4,1)}), s8[4194304]{0:T(1024)(128)(4,1)S(1)}, s32[]{:S(2)}) async-start(s8[6291456]{0:T(1024)(128)(4,1)} %bitcast.151), calls=%async_computation.6 | async-start | bytes 8388608
  185.3 6.0 %slice-start.1 = ((s8[6291456]{0:T(1024)(128)(4,1)}), s8[2097152]{0:T(1024)(128)(4,1)S(1)}, s32[]{:S(2)}) async-start(s8[6291456]{0:T(1024)(128)(4,1)} %bitcast.151), calls=%async_computation.7 | async-start | bytes 4194304
  190.4 3.5 copy-start.2
  243.8 96.6 %all-to-all-start = ((bf16[64,2,384]{2,1,0:T(2,128)(2,1)}), bf16[64,2,384]{2,1,0:T(2,128)(2,1)S(1)}, u32[]{:S(2)}, u32[]{:S(2)}) async-start(bf16[64,2,384]{2,1,0:T(2,128)(2,1)} %reshape.688), calls=%async_computation | async-start | bytes 196608 | tf_op jit(solution)/shard_map/all_to_all | solution.py:187
  250.2 24.9 %copy-start.5 = (bf16[64,768]{1,0:T(8,128)(2,1)S(1)}, bf16[64,768]{1,0:T(8,128)(2,1)}, u32[]{:S(2)}) copy-start(bf16[64,768]{1,0:T(8,128)(2,1)} %param.11) | copy-start | bytes 294916
  350.5 6.9 %copy-start.4 = (bf16[64,768]{1,0:T(8,128)(2,1)S(1)}, bf16[64,768]{1,0:T(8,128)(2,1)}, u32[]{:S(2)}) copy-start(bf16[64,768]{1,0:T(8,128)(2,1)} %param.12) | copy-start | bytes 294916
  357.4 10.6 %copy-start.1 = (bf16[32,768]{1,0:T(8,128)(2,1)S(1)}, bf16[32,768]{1,0:T(8,128)(2,1)}, u32[]{:S(2)}) copy-start(bf16[32,768]{1,0:T(8,128)(2,1)} %param.13) | copy-start | bytes 147460
Sparse Core Ops, SparseCore 0:
  10.8 85.2 all-gather.6
  98.9 77.6 all-gather.8
  179.3 78.1 all-gather.10
  260.7 78.3 all-gather.12
where the time goes:
time: 376 us; the launch traced here: 375 us
  waiting for transfers between devices  122 us (32%)
  blocking collectives  117 us (31%)
  local copies, waits for them, and re-layouts  48.4 us (13%)
  matrix products  43.1 us (11%)
  starting transfers between devices  15 us (4%)
  other arithmetic  14.4 us (4%)
  between operations  14.1 us (4%)
    all_gather x1, waiting for transfers between devices, body(): lax.all_gather(values, 'seq', axis=0, tiled=True)  71.7 us
    all_gather x1, blocking collectives, body(): lax.all_gather(row_delta, 'seq', axis=0, tiled=True)  44.8 us
    all_gather x1, blocking collectives, body(): lax.all_gather(log_total.T, 'seq', axis=0, tiled=True)  42.6 us
    all_gather x1, waiting for transfers between devices, body(): lax.all_gather(keys, 'seq', axis=0, tiled=True)  37.2 us
    unnamed x1, blocking collectives  20.8 us
    dot_general x1, matrix products, query_side(): jnp.einsum('hqk,khd->qhd', score_grad, split_heads(key_rows, head_count),...  10.8 us
    dot_general x1, matrix products, key_side(): jnp.einsum('hkq,qhd->khd', score_grad, query_heads, preferred_element_typ...  9.71 us
    psum x1, blocking collectives, gate_sum(): return lax.psum(partial_sum, 'tp')  8.82 us
  transfers between devices with their start and end apart: 6, of which 4 were waited for; matrix products, arithmetic and copies ran while one was open for 21% of the time, Pallas kernels for 0%

commit v1 on v0

v1 whole, which is shorter than its diff:
```python
import functools

import jax
import jax.numpy as jnp
from jax import lax
from jax.experimental import pallas as pl
from jax.experimental.pallas import tpu as pltpu
from jax.sharding import PartitionSpec as P

HD = 128
SEQ = 64
CAP = 64
TOK = 256
WPH = 8
CLS = 256
MSG = 16
SCALE = HD ** -0.5
MESH = pl.DeviceIdType.MESH
BF16, F32, I32 = jnp.bfloat16, jnp.float32, jnp.int32


def iota(shape, axis):
    return lax.broadcasted_iota(I32, shape, axis)


def onehot(hit):
    return jnp.where(hit, 1.0, 0.0).astype(BF16)


def dot(a, b):
    return lax.dot_general(a, b, (((1,), (0,)), ((), ())), preferred_element_type=F32)


def dot_nt(a, b):
    return lax.dot_general(a, b, (((1,), (1,)), ((), ())), preferred_element_type=F32)


def dot_tn(a, b):
    return lax.dot_general(a, b, (((0,), (0,)), ((), ())), preferred_element_type=F32)


def place_of(head, cls):
    z = head + head // 3
    return (cls // 2) * 16 + z * 2 + lax.rem(cls, 2)


def remote(src, dst, send, recv, device):
    return pltpu.make_async_remote_copy(
        src_ref=src, dst_ref=dst, send_sem=send, recv_sem=recv, device_id=device, device_id_type=MESH
    )


def kernel(
    n_tp,
    heads,
    picked_ref,
    perm_ref,
    logit_ref,
    q_ref,
    k_ref,
    v_ref,
    d_ref,
    gated_ref,
    dq_ref,
    dk_ref,
    dv_ref,
    router_ref,
    cnt_out,
    cnt,
    msg,
    rows,
    own,
    kv,
    dsend,
    dcls,
    sbuf,
    pbuf,
    part,
    psum,
    gsend,
    gchk,
    gg,
    back,
    home,
    send_sem,
    recv_sem,
    kv_sem,
    ps_sem,
    loc_sem,
):
    me = lax.axis_index("seq")
    tp = lax.axis_index("tp")
    z = lax.rem(lax.div(me, 2), 8)
    core = lax.rem(me, 2)
    x = lax.div(me, 16)
    is_worker = lax.rem(z, 4) < 3
    head = z - lax.div(z, 4)
    cls = x * 2 + core
    slot = head * WPH + cls
    workers = heads * WPH

    barrier = pltpu.get_barrier_semaphore()

    def greet(n, carry):
        pl.semaphore_signal(barrier, inc=1, device_id={"seq": lax.rem(me + n, SEQ)}, device_id_type=MESH)
        return carry

    lax.fori_loop(1, SEQ, greet, 0)
    for n in range(1, n_tp):
        pl.semaphore_signal(barrier, inc=1, device_id={"tp": lax.rem(tp + n, n_tp)}, device_id_type=MESH)

    picked = picked_ref[...]
    count = jnp.sum(jnp.where(picked >= 0, 1, 0), axis=1, keepdims=True)
    cnt_out[...] = jnp.broadcast_to(count, (1, 128))
    pl.semaphore_wait(barrier, SEQ - 1 + n_tp - 1)

    def send_count(n, carry):
        remote(cnt_out, cnt.at[me], send_sem.at[0], recv_sem.at[0], {"seq": lax.rem(me + n, SEQ)}).start()
        return carry

    lax.fori_loop(1, SEQ, send_count, 0)
    cnt[me] = cnt_out[...]

    eye = iota((CAP, CAP), 0) == iota((CAP, CAP), 1)
    picked_col = jnp.sum(jnp.where(eye, jnp.broadcast_to(picked, (CAP, CAP)), 0), axis=1, keepdims=True)
    spots = jnp.broadcast_to(picked_col - me * TOK, (CAP, TOK)) == iota((CAP, TOK), 1)
    logits = jnp.broadcast_to(logit_ref[...].astype(F32), (CAP, TOK))
    logit_col = jnp.sum(jnp.where(spots, logits, 0.0), axis=1, keepdims=True)
    gate_col = 1.0 / (1.0 + jnp.exp(-logit_col))
    spread = jnp.where(iota((CAP, 128), 1) == (iota((CAP, 128), 0) >> 3), jnp.broadcast_to(logit_col, (CAP, 128)), 0.0)
    spread = spread.astype(BF16)

    remote(cnt.at[pl.ds(0, SEQ - 1)], cnt.at[pl.ds(0, SEQ - 1)], send_sem.at[0], recv_sem.at[0], {"seq": me}).wait_recv()
    counts = jnp.sum(cnt[...], axis=1)
    start = jnp.sum(jnp.where(iota((SEQ, 128), 0) < me, counts, 0), axis=0, keepdims=True)

    n_out = iota((WPH * MSG, 128), 0)
    t_out = n_out & 15
    turn = ((n_out >> 4) - start) & 7
    src = iota((WPH * MSG, 128), 1)
    pick_left = onehot(src == 8 * t_out + turn)
    right_at = jnp.where(t_out < 8, 8 * t_out + turn, jnp.where(t_out < 12, CAP + 4 * (n_out >> 4) + t_out - 8, -1))
    pick_right = onehot(src == right_at)
    src64 = iota((WPH * MSG, CAP), 1)
    pick_logit = onehot((t_out[:, :CAP] == 12) & ((src64 & 7) == turn[:, :CAP]))
    logit_rows = dot(pick_logit, spread)
    for k in range(heads):
        cols = slice(k * HD, (k + 1) * HD)
        left = dot(pick_left, jnp.concatenate([q_ref[:, cols], k_ref[:, cols]], axis=0))
        fill = jnp.zeros((32, HD), BF16)
        right = dot(pick_right, jnp.concatenate([v_ref[:, cols], d_ref[:, cols], fill], axis=0)) + logit_rows
        both = jnp.concatenate([left, right], axis=1).astype(BF16)
        msg[pl.ds(k * WPH, WPH)] = both.reshape(WPH, MSG, 2 * HD)

    def send_rows(n, carry):
        w = lax.rem(n + me, workers)
        dst = place_of(lax.div(w, WPH), lax.rem(w, WPH))

        @pl.when(dst != me)
        def _():
            remote(msg.at[w], rows.at[me], send_sem.at[1], recv_sem.at[1], {"seq": dst}).start()

        return carry

    lax.fori_loop(0, workers, send_rows, 0)

    @pl.when(is_worker)
    def _():
        own_rows = pltpu.make_async_copy(msg.at[slot], rows.at[me], loc_sem.at[0])
        own_rows.start()

        n_row = iota((SEQ, SEQ * MSG), 1)
        below = jnp.concatenate([counts] * 8, axis=1)
        at_h = iota((SEQ, SEQ * MSG), 0)
        start_n = jnp.sum(jnp.where(at_h < (n_row >> 4), below, 0), axis=0, keepdims=True)
        end_n = jnp.sum(jnp.where(at_h <= (n_row >> 4), below, 0), axis=0, keepdims=True)
        t_n = iota((1, SEQ * MSG), 1) & 15
        p_n = ((start_n - cls + 7) >> 3) + (t_n & 7)
        live_n = p_n < ((end_n - cls + 7) >> 3)
        q_at = jnp.where(live_n & (t_n < 8), p_n, -1)
        k_at = jnp.where(live_n & (t_n >= 8), p_n, -1)
        p_sub = iota((CLS, SEQ * MSG), 0)
        take_q = onehot(p_sub == q_at)
        take_k = onehot(p_sub == k_at)
        m_sub = iota((CLS, SEQ), 0)
        residue_m = 8 * (m_sub & 7) + (m_sub >> 5)
        perm = jnp.broadcast_to(perm_ref[...], (CLS, SEQ))
        owner_m = jnp.sum(jnp.where(iota((CLS, SEQ), 1) == residue_m, perm, 0), axis=1, keepdims=True)
        d_at = MSG * owner_m + 8 + ((iota((CLS, 1), 0) & 31) >> 3)
        take_d = onehot(iota((CLS, SEQ * MSG), 1) == d_at)
        take_l = onehot(n_row == MSG * at_h + 12)

        tri = onehot(iota((SEQ, SEQ), 1) < iota((SEQ, SEQ), 0))
        starts = dot(tri, counts.astype(BF16)).astype(I32)
        base = (starts - cls + 7) >> 3
        after = (starts + counts - cls + 7) >> 3
        base2 = jnp.concatenate([base, base], axis=1)
        after2 = jnp.concatenate([after, after], axis=1)
        p_lane = iota((SEQ, CLS), 1)
        of_home = (base2 <= p_lane) & (p_lane < after2)
        lane_p = jnp.sum(jnp.where(of_home, p_lane - base2, 0), axis=0, keepdims=True)
        lanes = onehot(iota((128, CLS), 0) == lane_p)

        remote(rows.at[pl.ds(0, SEQ - 1)], rows.at[pl.ds(0, SEQ - 1)], send_sem.at[1], recv_sem.at[1], {"seq": me}).wait_recv()
        own_rows.wait()
        got = rows[...].reshape(SEQ * MSG, 2 * HD)
        qv = dot(take_q, got).astype(BF16)
        kc = dot(take_k, got[:, :HD]).astype(BF16)
        own[0] = qv[:, :HD]
        kv[cls] = jnp.concatenate([kc, qv[:, HD:]], axis=1)
        dsend[...] = dot(take_d, got[:, HD:]).astype(BF16).reshape(WPH, 32, HD)

        def send_kv(n, carry):
            to = lax.rem(cls + n, WPH)
            dst = {"seq": place_of(head, to)}
            remote(kv.at[cls], kv.at[cls], send_sem.at[2], kv_sem.at[cls], dst).start()
            remote(dsend.at[to], dcls.at[cls], send_sem.at[3], recv_sem.at[2], dst).start()
            return carry

        lax.fori_loop(1, WPH, send_kv, 0)
        dcls[cls] = dsend[cls]

        logit_h = dot(take_l, got[:, HD:]).astype(BF16)
        logit_p = jnp.sum(jnp.where(of_home, dot(logit_h, lanes), 0.0), axis=0, keepdims=True)
        gate = 1.0 / (1.0 + jnp.exp(-logit_p))

        q = own[0]
        top = jnp.full((1, CLS), -jnp.inf, F32)
        k_sub, q_lane = iota((CLS, CLS), 0), iota((CLS, CLS), 1)
        for n in range(WPH):
            other = lax.rem(cls + n, WPH)
            if n:
                remote(kv.at[other], kv.at[other], send_sem.at[2], kv_sem.at[other], {"seq": me}).wait_recv()
            later = jnp.where(other > cls, 1, 0)
            s = dot_nt(kv[other, :, :HD], q) * SCALE
            s = jnp.where(k_sub + later <= q_lane, s, -1e30)
            sbuf[n] = s
            top = jnp.maximum(top, jnp.max(s, axis=0, keepdims=True))
        total = jnp.zeros((1, CLS), F32)
        for n in range(WPH):
            e = jnp.exp(sbuf[n] - top)
            sbuf[n] = e
            total = total + jnp.sum(e, axis=0, keepdims=True)
        inv = 1.0 / total
        out_t = jnp.zeros((HD, CLS), F32)
        for n in range(WPH):
            other = lax.rem(cls + n, WPH)
            w = sbuf[n] * inv
            sbuf[n] = w
            wb = w.astype(BF16)
            pbuf[n] = wb
            out_t = out_t + dot_tn(kv[other, :, HD:], wb)

        remote(dcls.at[pl.ds(0, WPH - 1)], dcls.at[pl.ds(0, WPH - 1)], send_sem.at[3], recv_sem.at[2], {"seq": me}).wait_recv()
        dy_t = dcls[...].reshape(CLS, HD).astype(F32).T
        dor_t = (dy_t * gate).astype(BF16).astype(F32)
        dor = dor_t.T.astype(BF16)
        delta = jnp.sum(dor_t * out_t, axis=0, keepdims=True)
        gate_grad = jnp.sum(dy_t * out_t, axis=0, keepdims=True)
        gsend[...] = (out_t * gate).T.astype(BF16).reshape(WPH, 32, HD)
        gg[tp] = jnp.broadcast_to(gate_grad, (8, CLS))

        def send_gated(n, carry):
            to = lax.rem(cls + n, WPH)
            remote(gsend.at[to], gchk.at[cls], send_sem.at[4], recv_sem.at[3], {"seq": place_of(head, to)}).start()
            return carry

        lax.fori_loop(1, WPH, send_gated, 0)
        gchk[cls] = gsend[cls]
        for n in range(1, n_tp):
            remote(gg.at[tp], gg.at[tp], send_sem.at[5], recv_sem.at[4], {"tp": lax.rem(tp + n, n_tp)}).start()

        dq_t = jnp.zeros((HD, CLS), F32)
        mine = None
        for n in list(range(1, WPH)) + [0]:
            other = lax.rem(cls + n, WPH)
            dp = dot_nt(kv[other, :, HD:], dor)
            ds = (sbuf[n] * (dp - delta)).astype(BF16)
            dq_t = dq_t + dot_tn(kv[other, :, :HD], ds)
            grads = jnp.concatenate([dot(ds, q) * SCALE, dot(pbuf[n], dor)], axis=1)
            if n:
                part[n] = grads.astype(BF16)
                remote(part.at[n], psum.at[cls], send_sem.at[6], ps_sem.at[cls], {"seq": place_of(head, other)}).start()
            else:
                mine = grads
        dqc = (dq_t * SCALE).T.astype(BF16)

        n_sub = iota((SEQ * MSG, SEQ), 0)
        rep = onehot((n_sub >> 4) == iota((SEQ * MSG, SEQ), 1))
        perm_o = jnp.broadcast_to(perm_ref[...], (SEQ, SEQ))
        res_o = jnp.sum(jnp.where(perm_o == iota((SEQ, SEQ), 0), iota((SEQ, SEQ), 1), 0), axis=1, keepdims=True)
        three = jnp.concatenate([base, after, jnp.broadcast_to(res_o, (SEQ, 128))], axis=1).astype(F32).astype(BF16)
        wide = dot(rep, three).astype(I32)
        t_col = iota((SEQ * MSG, 128), 0) & 15
        p_col = wide[:, :128] + (t_col & 7)
        live_col = p_col < wide[:, 128:256]
        res_col = wide[:, 256:]
        q_to = jnp.where(live_col & (t_col < 8), p_col, -1)
        k_to = jnp.where(live_col & (t_col >= 8), p_col, -1)
        o_to = jnp.where((t_col >= 8) & (t_col < 12), 32 * (res_col & 7) + 8 * (t_col - 8) + (res_col >> 3), -1)
        p_at = iota((SEQ * MSG, CLS), 1)
        put_q = onehot(p_at == jnp.concatenate([q_to, q_to], axis=1))
        put_k = onehot(p_at == jnp.concatenate([k_to, k_to], axis=1))
        put_o = onehot(p_at == jnp.concatenate([o_to, o_to], axis=1))
        put_g = onehot(iota((SEQ * MSG, SEQ), 0) == MSG * iota((SEQ * MSG, SEQ), 1) + 12)

        if n_tp > 1:
            others = gg.at[pl.ds(0, n_tp - 1)]
            remote(others, others, send_sem.at[5], recv_sem.at[4], {"seq": me}).wait_recv()
        gate_sum = jnp.sum(gg[...], axis=0)[0:1]
        gg_home = dot_nt(jnp.where(of_home, gate_sum, 0.0).astype(BF16), lanes).astype(BF16)
        remote(gchk.at[pl.ds(0, WPH - 1)], gchk.at[pl.ds(0, WPH - 1)], send_sem.at[4], recv_sem.at[3], {"seq": me}).wait_recv()
        right_rows = dot(put_g, gg_home) + dot(put_o, gchk[...].reshape(CLS, HD))
        for n in range(1, WPH):
            other = lax.rem(cls + n, WPH)
            remote(psum.at[other], psum.at[other], send_sem.at[6], ps_sem.at[other], {"seq": me}).wait_recv()
            mine = mine + psum[other].astype(F32)
        mine = mine.astype(BF16)
        qv_rows = dot(put_q, jnp.concatenate([dqc, mine[:, HD:]], axis=1))
        k_rows = dot(put_k, mine[:, :HD])
        full = jnp.concatenate([qv_rows[:, :HD] + k_rows, qv_rows[:, HD:] + right_rows], axis=1)
        back[...] = full.astype(BF16).reshape(SEQ, MSG, 2 * HD)

        def send_back(n, carry):
            to = lax.rem(me + n, SEQ)
            remote(back.at[to], home.at[slot], send_sem.at[7], recv_sem.at[5], {"seq": to}).start()
            return carry

        lax.fori_loop(1, SEQ, send_back, 0)
        own_back = pltpu.make_async_copy(back.at[me], home.at[slot], loc_sem.at[1])
        own_back.start()

        remote(rows.at[pl.ds(0, workers - 1)], rows.at[pl.ds(0, workers - 1)], send_sem.at[1], recv_sem.at[1], {"seq": me}).wait_send()
        remote(kv.at[pl.ds(0, WPH - 1)], kv.at[pl.ds(0, WPH - 1)], send_sem.at[2], kv_sem.at[0], {"seq": me}).wait_send()
        remote(dsend.at[pl.ds(0, WPH - 1)], dcls.at[pl.ds(0, WPH - 1)], send_sem.at[3], recv_sem.at[2], {"seq": me}).wait_send()
        remote(gsend.at[pl.ds(0, WPH - 1)], gchk.at[pl.ds(0, WPH - 1)], send_sem.at[4], recv_sem.at[3], {"seq": me}).wait_send()
        if n_tp > 1:
            remote(others, others, send_sem.at[5], recv_sem.at[4], {"seq": me}).wait_send()
        remote(part.at[pl.ds(0, WPH - 1)], part.at[pl.ds(0, WPH - 1)], send_sem.at[6], ps_sem.at[0], {"seq": me}).wait_send()
        remote(back.at[pl.ds(0, SEQ - 1)], back.at[pl.ds(0, SEQ - 1)], send_sem.at[7], recv_sem.at[5], {"seq": me}).wait_send()
        own_back.wait()
        remote(home.at[pl.ds(0, workers - 1)], home.at[pl.ds(0, workers - 1)], send_sem.at[7], recv_sem.at[5], {"seq": me}).wait_recv()

    @pl.when(jnp.logical_not(is_worker))
    def _():
        remote(msg, msg, send_sem.at[1], recv_sem.at[1], {"seq": me}).wait_send()
        remote(home, home, send_sem.at[7], recv_sem.at[5], {"seq": me}).wait_recv()

    j = iota((256, 128), 0)
    col = iota((256, 128), 1)
    slot_j = j & 63
    from_cls = MSG * ((start + slot_j) & 7)
    at = jnp.where(j < 64, from_cls + (slot_j >> 3), from_cls + 8 + (slot_j >> 3))
    at = jnp.where(j < 128, at, from_cls + 12)
    at = jnp.where(j < 192, at, jnp.where(j < 224, MSG * (slot_j >> 2) + 8 + (slot_j & 3), -1))
    take = onehot(col == at)
    gate_rows = jnp.zeros((CAP, HD), F32)
    for k in range(heads):
        cols = slice(k * HD, (k + 1) * HD)
        res = dot(take, home[pl.ds(k * WPH, WPH)].reshape(WPH * MSG, 2 * HD))
        dq_ref[:, cols] = res[0:64, :HD].astype(BF16)
        dk_ref[:, cols] = res[64:128, :HD].astype(BF16)
        dv_ref[:, cols] = res[0:64, HD:].astype(BF16)
        gated_ref[:, cols] = res[192:224, HD:].astype(BF16)
        gate_rows = gate_rows + res[128:192, HD:]
    mine_lane = iota((CAP, HD), 1) == (iota((CAP, HD), 0) >> 3)
    gate_grad = jnp.sum(jnp.where(mine_lane, gate_rows, 0.0), axis=1, keepdims=True)
    logit_grad = gate_grad * gate_col * (1.0 - gate_col)
    router_ref[...] = jnp.sum(jnp.where(spots, jnp.broadcast_to(logit_grad, (CAP, TOK)), 0.0), axis=0, keepdims=True)
    remote(cnt.at[pl.ds(0, SEQ - 1)], cnt.at[pl.ds(0, SEQ - 1)], send_sem.at[0], recv_sem.at[0], {"seq": me}).wait_send()


def body(picked, owner_perm, router_logit, queries, keys, values, out_grad):
    n_tp = lax.axis_size("tp")
    heads = queries.shape[1] // HD
    width = heads * HD
    workers = heads * WPH
    vmem = pl.BlockSpec(memory_space=pltpu.VMEM)
    dma = pltpu.SemaphoreType.DMA
    gated, dq, dk, dv, router = pl.pallas_call(
        functools.partial(kernel, n_tp, heads),
        out_shape=(
            jax.ShapeDtypeStruct((out_grad.shape[0], width), BF16),
            jax.ShapeDtypeStruct((CAP, width), BF16),
            jax.ShapeDtypeStruct((CAP, width), BF16),
            jax.ShapeDtypeStruct((CAP, width), BF16),
            jax.ShapeDtypeStruct((1, TOK), F32),
        ),
        in_specs=[vmem] * 7,
        out_specs=[vmem] * 5,
        scratch_shapes=[
            pltpu.VMEM((1, 128), I32),
            pltpu.VMEM((SEQ, 1, 128), I32),
            pltpu.VMEM((workers, MSG, 2 * HD), BF16),
            pltpu.VMEM((SEQ, MSG, 2 * HD), BF16),
            pltpu.VMEM((1, CLS, HD), BF16),
            pltpu.VMEM((WPH, CLS, 2 * HD), BF16),
            pltpu.VMEM((WPH, 32, HD), BF16),
            pltpu.VMEM((WPH, 32, HD), BF16),
            pltpu.VMEM((WPH, CLS, CLS), F32),
            pltpu.VMEM((WPH, CLS, CLS), BF16),
            pltpu.VMEM((WPH, CLS, 2 * HD), BF16),
            pltpu.VMEM((WPH, CLS, 2 * HD), BF16),
            pltpu.VMEM((WPH, 32, HD), BF16),
            pltpu.VMEM((WPH, 32, HD), BF16),
            pltpu.VMEM((n_tp, 8, CLS), F32),
            pltpu.VMEM((SEQ, MSG, 2 * HD), BF16),
            pltpu.VMEM((workers, MSG, 2 * HD), BF16),
            dma((8,)),
            dma((6,)),
            dma((WPH,)),
            dma((WPH,)),
            dma((2,)),
        ],
        compiler_params=pltpu.CompilerParams(
            collective_id=0, has_side_effects=True, vmem_limit_bytes=48 * 1024 * 1024
        ),
    )(
        picked.reshape(1, CAP),
        owner_perm.reshape(1, SEQ),
        router_logit.reshape(1, TOK),
        queries,
        keys,
        values,
        out_grad,
    )
    return gated, dq, dk, dv, router.reshape(TOK)


def solution(mesh):
    return jax.shard_map(
        body,
        mesh=mesh,
        in_specs=(P("seq"), P(), P("seq"), P("seq", "tp"), P("seq", "tp"), P("seq", "tp"), P("seq", "tp")),
        out_specs=(P("seq", "tp"), P("seq", "tp"), P("seq", "tp"), P("seq", "tp"), P("seq")),
        check_vma=False,
    )
```

time: 376 us -> 85.1 us (0.23)
  waiting for transfers between devices: 122 us -> 0 us
  blocking collectives: 117 us -> 0 us
  Pallas kernels: 0 us -> 76.3 us
  matrix products: 43.1 us -> 0 us
  local copies, waits for them, and re-layouts: 48.4 us -> 7.9 us
  starting transfers between devices: 15 us -> 0 us
  other arithmetic: 14.4 us -> 0 us
  between operations: 14.1 us -> 0.66 us
    all_gather x4 -> x0, waiting for transfers between devices: 116 us -> none  [the longest x1 71.7 us: body(): lax.all_gather(values, 'seq', axis=0, tiled=True)]
    all_gather x2 -> x0, blocking collectives: 87.4 us -> none  [the longest x1 44.8 us: body(): lax.all_gather(row_delta, 'seq', axis=0, tiled=True)]
    pallas_call x0 -> x1, Pallas kernels: none -> 76.3 us  [body(): pl.pallas_call(functools.partial(kernel, n_tp, heads), out_shape=(jax.Sha...]
    dot_general x6 -> x0, matrix products: 43.1 us -> none  [the longest x1 10.8 us: query_side(): jnp.einsum('hqk,khd->qhd', score_grad, split_heads(key_rows, head_count),...]
    all_gather x6 -> x0, local copies, waits for them, and re-layouts: 35.1 us -> none  [the longest x1 8.78 us: body(): lax.all_gather(values, 'seq', axis=0, tiled=True)]
    unnamed x1 -> x0, blocking collectives: 20.8 us -> none
    all_to_all x2 -> x0, starting transfers between devices: 14.9 us -> none  [the longest x1 8.46 us: body(): lax.all_to_all(pick_rows(out_grad, spot_back, back_keep), 'seq', split_ax...]
    psum x1 -> x0, blocking collectives: 8.82 us -> none  [gate_sum(): return lax.psum(partial_sum, 'tp')]
  transfers between devices with their start and end apart: 6 -> 0, of which waited for: 4 -> 0; matrix products, arithmetic and copies ran while one was open for 21% -> 0% of each run, Pallas kernels for 0% -> 0%
where the time goes in v1:
time: 85.1 us; the launch traced here: 84.9 us
  Pallas kernels  76.3 us (90%)
  local copies, waits for them, and re-layouts  7.9 us (9%)
    pallas_call x1, Pallas kernels, body(): pl.pallas_call(functools.partial(kernel, n_tp, heads), out_shape=(jax.Sha...  76.3 us
    unnamed x19, local copies, waits for them, and re-layouts  7.89 us

profile of v1, /device:TPU:1, one launch (start us, length us, event | category | flops | bytes accessed | tf_op | source)
XLA Modules:
  0.0 84.9 jit_solution(2218619397280452371)
XLA Ops:
  0.6 0.0 copy-start.6
  0.6 0.6 copy-done.6
  1.3 0.0 copy-start.4
  1.3 0.0 copy-start.5
  1.3 0.6 copy-done.4
  1.9 0.0 copy-done.5
  2.0 0.0 copy-start
  2.0 0.9 %copy-done = bf16[64,768]{1,0:T(8,128)(2,1)S(1)} copy-done((bf16[64,768]{1,0:T(8,128)(2,1)S(1)}, bf16[64,768]{1,0:T(8,128)(2,1)}, u32[]{:S(2)}) %copy-start) | copy-done | bytes 98328
  2.9 0.0 copy-start.1
  2.9 0.9 %copy-done.1 = bf16[64,768]{1,0:T(8,128)(2,1)S(1)} copy-done((bf16[64,768]{1,0:T(8,128)(2,1)S(1)}, bf16[64,768]{1,0:T(8,128)(2,1)}, u32[]{:S(2)}) %copy-start.1) | copy-done | bytes 98328
  3.7 0.0 copy-start.2
  3.7 0.9 %copy-done.2 = bf16[64,768]{1,0:T(8,128)(2,1)S(1)} copy-done((bf16[64,768]{1,0:T(8,128)(2,1)S(1)}, bf16[64,768]{1,0:T(8,128)(2,1)}, u32[]{:S(2)}) %copy-start.2) | copy-done | bytes 98328
  4.6 0.0 copy-start.3
  4.6 0.8 copy-done.3
  5.4 76.3 %shard_map.110 = (bf16[32,768]{1,0:T(8,128)(2,1)S(1)}, bf16[64,768]{1,0:T(8,128)(2,1)S(1)}, bf16[64,768]{1,0:T(8,128)(2,1)S(1)}, bf16[64,768]{1,0:T(8,128)(2,1)S(1)}, f32[1,256]{1,0:T(1,128)S(1)}) custom-call(s32[1,64]{1,0:T(1,128)S(1)} %bitcast.4, s32[1,64]{1,0:T(1,128)S(1)} %bitcast.5, bf16[1,256]{1,0:T(2,128)(2,1)S(1)} %reshape.24.logit_ref, ...), custom_call_target="tpu_custom_call" | custom-call | tf_op jit(solution)/shard_map/pallas_call | solution.py:380
  81.8 0.6 copy.17
  82.4 0.6 copy.18
  83.0 0.6 copy.19
  83.7 0.6 copy.20
  84.3 0.6 copy.21
  (1 shorter events, 0.0 us)
Async XLA Ops:
  0.6 0.7 copy-start.6
  1.3 0.7 copy-start.4
  1.3 0.7 copy-start.5
  2.0 0.9 %copy-start = (bf16[64,768]{1,0:T(8,128)(2,1)S(1)}, bf16[64,768]{1,0:T(8,128)(2,1)}, u32[]{:S(2)}) copy-start(bf16[64,768]{1,0:T(8,128)(2,1)} %q_ref.1) | copy-start | bytes 294916
  2.9 0.9 %copy-start.1 = (bf16[64,768]{1,0:T(8,128)(2,1)S(1)}, bf16[64,768]{1,0:T(8,128)(2,1)}, u32[]{:S(2)}) copy-start(bf16[64,768]{1,0:T(8,128)(2,1)} %k_ref.1) | copy-start | bytes 294916
  3.7 0.9 %copy-start.2 = (bf16[64,768]{1,0:T(8,128)(2,1)S(1)}, bf16[64,768]{1,0:T(8,128)(2,1)}, u32[]{:S(2)}) copy-start(bf16[64,768]{1,0:T(8,128)(2,1)} %v_ref.1) | copy-start | bytes 294916
  4.6 0.8 copy-start.3

commit v2 on v1

v2 whole, which is shorter than its diff:
```python
import functools

import jax
import jax.numpy as jnp
from jax import lax
from jax.experimental import pallas as pl
from jax.experimental.pallas import tpu as pltpu
from jax.sharding import PartitionSpec as P

HD = 128
SEQ = 64
CAP = 64
TOK = 256
WPH = 8
CLS = 256
MSG = 16
SCALE = HD ** -0.5
MESH = pl.DeviceIdType.MESH
BF16, F32, I32 = jnp.bfloat16, jnp.float32, jnp.int32


def iota(shape, axis):
    return lax.broadcasted_iota(I32, shape, axis)


def onehot(hit):
    return jnp.where(hit, 1.0, 0.0).astype(BF16)


def dot(a, b):
    return lax.dot_general(a, b, (((1,), (0,)), ((), ())), preferred_element_type=F32)


def dot_nt(a, b):
    return lax.dot_general(a, b, (((1,), (1,)), ((), ())), preferred_element_type=F32)


def dot_tn(a, b):
    return lax.dot_general(a, b, (((0,), (0,)), ((), ())), preferred_element_type=F32)


def place_of(head, cls):
    z = head + head // 3
    return (cls // 2) * 16 + z * 2 + lax.rem(cls, 2)


def remote(src, dst, send, recv, device):
    return pltpu.make_async_remote_copy(
        src_ref=src, dst_ref=dst, send_sem=send, recv_sem=recv, device_id=device, device_id_type=MESH
    )


def find_logits(me, picked, logits):
    eye = iota((CAP, CAP), 0) == iota((CAP, CAP), 1)
    picked_col = jnp.sum(jnp.where(eye, jnp.broadcast_to(picked, (CAP, CAP)), 0), axis=1, keepdims=True)
    spots = jnp.broadcast_to(picked_col - me * TOK, (CAP, TOK)) == iota((CAP, TOK), 1)
    halves = logits.astype(F32)
    wide = jnp.broadcast_to(jnp.concatenate([halves[0:1], halves[1:2]], axis=1), (CAP, TOK))
    return spots, jnp.sum(jnp.where(spots, wide, 0.0), axis=1, keepdims=True)


def kernel(
    n_tp,
    heads,
    picked_in,
    perm_in,
    logit_in,
    q_in,
    k_in,
    v_in,
    d_in,
    start_ref,
    home_a,
    home_b,
    picked_ref,
    perm_ref,
    logit_ref,
    q_ref,
    k_ref,
    v_ref,
    d_ref,
    cnt_out,
    cnt,
    msg_a,
    msg_b,
    rows_a,
    rows_b,
    k_all,
    v_all,
    dsend,
    dcls,
    put,
    sbuf,
    pbuf,
    part_k,
    part_v,
    pre_k,
    pre_v,
    sum_k,
    sum_v,
    gsend,
    gchk,
    gg,
    back_a,
    back_b,
    in_sem,
    send_sem,
    recv_sem,
    k_sem,
    v_sem,
    pre_k_sem,
    pre_v_sem,
    sum_k_sem,
    sum_v_sem,
    loc_sem,
):
    me = lax.axis_index("seq")
    tp = lax.axis_index("tp")
    z = lax.rem(lax.div(me, 2), 8)
    core = lax.rem(me, 2)
    x = lax.div(me, 16)
    is_worker = lax.rem(z, 4) < 3
    head = z - lax.div(z, 4)
    cls = x * 2 + core
    slot = head * WPH + cls
    workers = heads * WPH
    sibling = {"seq": me + 1 - 2 * core}

    loads = [
        pltpu.make_async_copy(src, dst, in_sem.at[n])
        for n, (src, dst) in enumerate(
            zip(
                (picked_in, perm_in, logit_in, k_in, v_in, q_in, d_in),
                (picked_ref, perm_ref, logit_ref, k_ref, v_ref, q_ref, d_ref),
            )
        )
    ]
    for load in loads:
        load.start()

    barrier = pltpu.get_barrier_semaphore()

    def greet(n, carry):
        pl.semaphore_signal(barrier, inc=1, device_id={"seq": lax.rem(me + n, SEQ)}, device_id_type=MESH)
        return carry

    lax.fori_loop(1, SEQ, greet, 0)
    for n in range(1, n_tp):
        pl.semaphore_signal(barrier, inc=1, device_id={"tp": lax.rem(tp + n, n_tp)}, device_id_type=MESH)

    loads[0].wait()
    picked = picked_ref[...]
    count = jnp.sum(jnp.where(picked >= 0, 1, 0), axis=1, keepdims=True)
    cnt_out[...] = jnp.broadcast_to(count, (1, 128))
    pl.semaphore_wait(barrier, SEQ - 1 + n_tp - 1)

    def send_count(n, carry):
        remote(cnt_out, cnt.at[me], send_sem.at[0], recv_sem.at[0], {"seq": lax.rem(me + n, SEQ)}).start()
        return carry

    lax.fori_loop(1, SEQ, send_count, 0)
    cnt[me] = cnt_out[...]

    for load in loads[1:]:
        load.wait()
    spots, logit_col = find_logits(me, picked, logit_ref[...])
    spread = jnp.where(iota((CAP, 128), 1) == (iota((CAP, 128), 0) >> 3), jnp.broadcast_to(logit_col, (CAP, 128)), 0.0)
    spread = spread.astype(BF16)
    fill = jnp.zeros((32, HD), BF16)

    counted = cnt.at[pl.ds(0, SEQ - 1)]
    remote(counted, counted, send_sem.at[0], recv_sem.at[0], sibling).wait_recv()
    counts = jnp.sum(cnt[...], axis=1)
    start = jnp.sum(jnp.where(iota((SEQ, 128), 0) < me, counts, 0), axis=0, keepdims=True)
    start_ref[...] = start

    n_out = iota((WPH * MSG, 128), 0)
    t_out = n_out & 15
    turn = ((n_out >> 4) - start) & 7
    src = iota((WPH * MSG, 128), 1)
    pick_a = onehot(src == 8 * t_out + turn)
    b_from = jnp.where(t_out < 8, 8 * t_out + turn, jnp.where(t_out < 12, CAP + 4 * (n_out >> 4) + t_out - 8, -1))
    pick_b = onehot(src == b_from)
    src64 = iota((WPH * MSG, CAP), 1)
    pick_logit = onehot((t_out[:, :CAP] == 12) & ((src64 & 7) == turn[:, :CAP]))

    def send_rows(msg, rows, sem):
        def send_one(n, carry):
            w = lax.rem(n + me, workers)
            dst = place_of(lax.div(w, WPH), lax.rem(w, WPH))

            @pl.when(dst != me)
            def _():
                remote(msg.at[w], rows.at[me], send_sem.at[sem], recv_sem.at[sem], {"seq": dst}).start()

            return carry

        lax.fori_loop(0, workers, send_one, 0)

    for k in range(heads):
        cols = slice(k * HD, (k + 1) * HD)
        both = dot(pick_a, jnp.concatenate([k_ref[:, cols], q_ref[:, cols]], axis=0))
        msg_a[pl.ds(k * WPH, WPH)] = both.astype(BF16).reshape(WPH, MSG, HD)
    send_rows(msg_a, rows_a, 1)
    logit_rows = dot(pick_logit, spread)
    for k in range(heads):
        cols = slice(k * HD, (k + 1) * HD)
        both = dot(pick_b, jnp.concatenate([v_ref[:, cols], d_ref[:, cols], fill], axis=0)) + logit_rows
        msg_b[pl.ds(k * WPH, WPH)] = both.astype(BF16).reshape(WPH, MSG, HD)
    send_rows(msg_b, rows_b, 2)

    @pl.when(is_worker)
    def _():
        left = []

        def gone(src, sem):
            left.append((src, sem))

        def done():
            for src, sem in left:
                remote(src, src, send_sem.at[sem], recv_sem.at[0], sibling).wait_send()

        def came(ref, sem):
            remote(ref, ref, send_sem.at[0], sem, sibling).wait_recv()

        own_a = pltpu.make_async_copy(msg_a.at[slot], rows_a.at[me], loc_sem.at[0])
        own_a.start()
        own_b = pltpu.make_async_copy(msg_b.at[slot], rows_b.at[me], loc_sem.at[1])
        own_b.start()
        gone(msg_a.at[pl.ds(0, workers - 1)], 1)
        gone(msg_b.at[pl.ds(0, workers - 1)], 2)

        def peer(n, flip):
            return lax.rem(x + n, 4) * 2 + (1 - core if flip else core)

        def send_all(ref, sems, sem):
            remote(ref.at[cls], ref.at[cls], send_sem.at[sem], sems.at[cls], sibling).start()
            for n in (1, 3, 2):
                dst = {"seq": place_of(head, peer(n, 0))}
                remote(ref.at[cls], ref.at[cls], send_sem.at[sem], sems.at[cls], dst).start()
            gone(ref.at[pl.ds(0, 4)], sem)

        def pass_on(ref, sems, sem, n):
            block = ref.at[peer(n, 0)]
            came(block, sems.at[peer(n, 0)])
            remote(block, block, send_sem.at[sem], sems.at[peer(n, 0)], sibling).start()

        n_row = iota((SEQ, SEQ * MSG), 1)
        below = jnp.concatenate([counts] * 8, axis=1)
        at_h = iota((SEQ, SEQ * MSG), 0)
        start_n = jnp.sum(jnp.where(at_h < (n_row >> 4), below, 0), axis=0, keepdims=True)
        end_n = jnp.sum(jnp.where(at_h <= (n_row >> 4), below, 0), axis=0, keepdims=True)
        t_n = iota((1, SEQ * MSG), 1) & 15
        p_n = ((start_n - cls + 7) >> 3) + (t_n & 7)
        live_n = p_n < ((end_n - cls + 7) >> 3)
        lo_at = jnp.where(live_n & (t_n < 8), p_n, -1)
        hi_at = jnp.where(live_n & (t_n >= 8), p_n, -1)
        p_sub = iota((CLS, SEQ * MSG), 0)
        take_lo = onehot(p_sub == lo_at)
        take_hi = onehot(p_sub == hi_at)

        came(rows_a.at[pl.ds(0, SEQ - 1)], recv_sem.at[1])
        own_a.wait()
        a_rows = rows_a[...].reshape(SEQ * MSG, HD)
        k_all[cls] = dot(take_lo, a_rows).astype(BF16)
        send_all(k_all, k_sem, 3)
        q = dot(take_hi, a_rows).astype(BF16)

        m_sub = iota((CLS, SEQ), 0)
        residue_m = 8 * (m_sub & 7) + (m_sub >> 5)
        perm = jnp.broadcast_to(perm_ref[...], (CLS, SEQ))
        owner_m = jnp.sum(jnp.where(iota((CLS, SEQ), 1) == residue_m, perm, 0), axis=1, keepdims=True)
        d_at = MSG * owner_m + 8 + ((iota((CLS, 1), 0) & 31) >> 3)
        take_d = onehot(iota((CLS, SEQ * MSG), 1) == d_at)
        take_l = onehot(n_row == MSG * at_h + 12)
        tri = onehot(iota((SEQ, SEQ), 1) < iota((SEQ, SEQ), 0))
        starts = dot(tri, counts.astype(BF16)).astype(I32)
        base = (starts - cls + 7) >> 3
        after = (starts + counts - cls + 7) >> 3
        base2 = jnp.concatenate([base, base], axis=1)
        after2 = jnp.concatenate([after, after], axis=1)
        p_lane = iota((SEQ, CLS), 1)
        of_home = (base2 <= p_lane) & (p_lane < after2)
        lane_p = jnp.sum(jnp.where(of_home, p_lane - base2, 0), axis=0, keepdims=True)
        lanes = onehot(iota((128, CLS), 0) == lane_p)

        n_sub = iota((SEQ * MSG, SEQ), 0)
        rep = onehot((n_sub >> 4) == iota((SEQ * MSG, SEQ), 1))
        perm_o = jnp.broadcast_to(perm_ref[...], (SEQ, SEQ))
        res_o = jnp.sum(jnp.where(perm_o == iota((SEQ, SEQ), 0), iota((SEQ, SEQ), 1), 0), axis=1, keepdims=True)
        three = jnp.concatenate([base, after, jnp.broadcast_to(res_o, (SEQ, 128))], axis=1).astype(F32).astype(BF16)
        wide = dot(rep, three).astype(I32)
        t_col = iota((SEQ * MSG, 128), 0) & 15
        p_col = wide[:, :128] + (t_col & 7)
        live_col = p_col < wide[:, 128:256]
        res_col = wide[:, 256:]
        lo_to = jnp.where(live_col & (t_col < 8), p_col, -1)
        hi_to = jnp.where(live_col & (t_col >= 8), p_col, -1)
        o_to = jnp.where((t_col >= 8) & (t_col < 12), 32 * (res_col & 7) + 8 * (t_col - 8) + (res_col >> 3), -1)
        p_at = iota((SEQ * MSG, CLS), 1)
        put[0] = onehot(p_at == jnp.concatenate([lo_to, lo_to], axis=1))
        put[1] = onehot(p_at == jnp.concatenate([hi_to, hi_to], axis=1))
        put[2] = onehot(p_at == jnp.concatenate([o_to, o_to], axis=1))
        put_g = onehot(iota((SEQ * MSG, SEQ), 0) == MSG * iota((SEQ * MSG, SEQ), 1) + 12)

        came(rows_b.at[pl.ds(0, SEQ - 1)], recv_sem.at[2])
        own_b.wait()
        b_rows = rows_b[...].reshape(SEQ * MSG, HD)
        v_all[cls] = dot(take_lo, b_rows).astype(BF16)
        send_all(v_all, v_sem, 4)
        dsend[...] = dot(take_d, b_rows).astype(BF16).reshape(WPH, 32, HD)

        def send_d(n, carry):
            to = lax.rem(cls + n, WPH)
            remote(dsend.at[to], dcls.at[cls], send_sem.at[6], recv_sem.at[3], {"seq": place_of(head, to)}).start()
            return carry

        lax.fori_loop(1, WPH, send_d, 0)
        dcls[cls] = dsend[cls]
        gone(dsend.at[pl.ds(0, WPH - 1)], 6)
        for n in (1, 3):
            pass_on(k_all, k_sem, 5, n)
        logit_h = dot(take_l, b_rows).astype(BF16)
        logit_p = jnp.sum(jnp.where(of_home, dot(logit_h, lanes), 0.0), axis=0, keepdims=True)
        gate = 1.0 / (1.0 + jnp.exp(-logit_p))

        top = jnp.full((1, CLS), -jnp.inf, F32)
        k_sub, q_lane = iota((CLS, CLS), 0), iota((CLS, CLS), 1)
        order = ((0, 0), (0, 1), (1, 0), (3, 0), (1, 1), (3, 1), (2, 0), (2, 1))
        for n, flip in order:
            other = peer(n, flip)
            if (n, flip) == (1, 0):
                pass_on(k_all, k_sem, 5, 2)
            if flip:
                came(k_all.at[other], k_sem.at[other])
            later = jnp.where(other > cls, 1, 0)
            s = dot_nt(k_all[other], q) * SCALE
            s = jnp.where(k_sub + later <= q_lane, s, -1e30)
            sbuf[2 * n + flip] = s
            top = jnp.maximum(top, jnp.max(s, axis=0, keepdims=True))
        gone(k_all.at[pl.ds(0, 3)], 5)
        total = jnp.zeros((1, CLS), F32)
        for n in range(WPH):
            e = jnp.exp(sbuf[n] - top)
            sbuf[n] = e
            total = total + jnp.sum(e, axis=0, keepdims=True)
        inv = 1.0 / total
        for n in range(WPH):
            w = sbuf[n] * inv
            sbuf[n] = w
            pbuf[n] = w.astype(BF16)

        came(dcls.at[pl.ds(0, WPH - 1)], recv_sem.at[3])
        dy_t = dcls[...].reshape(CLS, HD).astype(F32).T
        dor_t = (dy_t * gate).astype(BF16).astype(F32)
        dor = dor_t.T.astype(BF16)

        def to_sibling(grads, part, pre, sems, sem, n):
            part[2 * n + 1] = grads.astype(BF16)
            remote(part.at[2 * n + 1], pre.at[n], send_sem.at[sem], sems.at[n], sibling).start()

        def to_class(grads, part, pre, pre_sems, total, sems, sem, n):
            came(pre.at[n], pre_sems.at[n])
            grads = grads + pre[n].astype(F32)
            if n:
                part[2 * n] = grads.astype(BF16)
                dst = {"seq": place_of(head, peer(n, 0))}
                remote(part.at[2 * n], total.at[x], send_sem.at[sem], sems.at[x], dst).start()
            return grads

        def collect(mine, total, sems):
            for n in (1, 3, 2):
                there = lax.rem(x + n, 4)
                came(total.at[there], sems.at[there])
                mine = mine + total[there].astype(F32)
            return mine.astype(BF16)

        far_first = (2, 1, 3, 0)
        for n in far_first:
            to_sibling(dot(pbuf[2 * n + 1], dor), part_v, pre_v, pre_v_sem, 9, n)
        gone(part_v.at[pl.ds(0, 4)], 9)
        for n in (1, 3):
            pass_on(v_all, v_sem, 7, n)
        for n in far_first:
            mine_v = to_class(dot(pbuf[2 * n], dor), part_v, pre_v, pre_v_sem, sum_v, sum_v_sem, 10, n)
        gone(part_v.at[pl.ds(0, 3)], 10)
        pass_on(v_all, v_sem, 7, 2)
        gone(v_all.at[pl.ds(0, 3)], 7)
        out_t = jnp.zeros((HD, CLS), F32)
        for n, flip in order:
            other = peer(n, flip)
            if flip:
                came(v_all.at[other], v_sem.at[other])
            out_t = out_t + dot_tn(v_all[other], pbuf[2 * n + flip])
        delta = jnp.sum(dor_t * out_t, axis=0, keepdims=True)
        gate_grad = jnp.sum(dy_t * out_t, axis=0, keepdims=True)
        gsend[...] = (out_t * gate).T.astype(BF16).reshape(WPH, 32, HD)
        gg[tp] = jnp.broadcast_to(gate_grad, (8, CLS))

        def send_gated(n, carry):
            to = lax.rem(cls + n, WPH)
            remote(gsend.at[to], gchk.at[cls], send_sem.at[8], recv_sem.at[4], {"seq": place_of(head, to)}).start()
            return carry

        lax.fori_loop(1, WPH, send_gated, 0)
        gchk[cls] = gsend[cls]
        gone(gsend.at[pl.ds(0, WPH - 1)], 8)
        if n_tp > 1:
            for n in range(1, n_tp):
                remote(gg.at[tp], gg.at[tp], send_sem.at[13], recv_sem.at[5], {"tp": lax.rem(tp + n, n_tp)}).start()
            gone(gg.at[pl.ds(0, n_tp - 1)], 13)

        dq_t = jnp.zeros((HD, CLS), F32)
        for flip in (1, 0):
            for n in far_first:
                other = peer(n, flip)
                dp = dot_nt(v_all[other], dor)
                ds = (sbuf[2 * n + flip] * (dp - delta)).astype(BF16)
                dq_t = dq_t + dot_tn(k_all[other], ds)
                grads = dot(ds, q) * SCALE
                if flip:
                    to_sibling(grads, part_k, pre_k, pre_k_sem, 11, n)
                else:
                    mine_k = to_class(grads, part_k, pre_k, pre_k_sem, sum_k, sum_k_sem, 12, n)
        gone(part_k.at[pl.ds(0, 4)], 11)
        gone(part_k.at[pl.ds(0, 3)], 12)

        def send_back(back, home, sem):
            def send_one(n, carry):
                to = lax.rem(me + n, SEQ)
                remote(back.at[to], home.at[slot], send_sem.at[sem], recv_sem.at[sem - 8], {"seq": to}).start()
                return carry

            lax.fori_loop(1, SEQ, send_one, 0)
            gone(back.at[pl.ds(0, SEQ - 1)], sem)

        dqc = (dq_t * SCALE).T.astype(BF16)
        mine_v = collect(mine_v, sum_v, sum_v_sem)
        full = dot(put[0], mine_v) + dot(put[1], dqc)
        back_a[...] = full.astype(BF16).reshape(SEQ, MSG, HD)
        send_back(back_a, home_a, 14)
        own_a = pltpu.make_async_copy(back_a.at[me], home_a.at[slot], loc_sem.at[0])
        own_a.start()
        if n_tp > 1:
            came(gg.at[pl.ds(0, n_tp - 1)], recv_sem.at[5])
        gate_sum = jnp.sum(gg[...], axis=0)[0:1]
        gg_home = dot_nt(jnp.where(of_home, gate_sum, 0.0).astype(BF16), lanes).astype(BF16)
        came(gchk.at[pl.ds(0, WPH - 1)], recv_sem.at[4])
        rest = dot(put_g, gg_home) + dot(put[2], gchk[...].reshape(CLS, HD))
        mine_k = collect(mine_k, sum_k, sum_k_sem)
        full = dot(put[0], mine_k) + rest
        back_b[...] = full.astype(BF16).reshape(SEQ, MSG, HD)
        send_back(back_b, home_b, 15)
        own_b = pltpu.make_async_copy(back_b.at[me], home_b.at[slot], loc_sem.at[1])
        own_b.start()
        done()
        own_a.wait()
        own_b.wait()
        came(home_a.at[pl.ds(0, workers - 1)], recv_sem.at[6])
        came(home_b.at[pl.ds(0, workers - 1)], recv_sem.at[7])

    @pl.when(jnp.logical_not(is_worker))
    def _():
        remote(msg_a, msg_a, send_sem.at[1], recv_sem.at[1], sibling).wait_send()
        remote(msg_b, msg_b, send_sem.at[2], recv_sem.at[2], sibling).wait_send()
        remote(home_a, home_a, send_sem.at[14], recv_sem.at[6], sibling).wait_recv()
        remote(home_b, home_b, send_sem.at[15], recv_sem.at[7], sibling).wait_recv()

    remote(counted, counted, send_sem.at[0], recv_sem.at[0], sibling).wait_send()


def finish(
    heads, picked_ref, logit_ref, start_ref, home_a, home_b, gated_ref, dq_ref, dk_ref, dv_ref, router_ref
):
    me = lax.axis_index("seq")
    start = start_ref[...]
    spots, logit_col = find_logits(me, picked_ref[...], logit_ref[...])
    gate_col = 1.0 / (1.0 + jnp.exp(-logit_col))
    col = iota((CAP, 128), 1)
    j = iota((CAP, 128), 0)
    from_cls = MSG * ((start + j) & 7)
    lo = from_cls + (j >> 3)
    take_lo = col == lo
    take_hi = col == lo + 8
    take_g = col == from_cls + 12
    take_o = (col == MSG * (j >> 2) + 8 + (j & 3)) & (j < 32)
    take_a = jnp.concatenate([onehot(take_lo), onehot(take_hi)], axis=0)
    take_b = jnp.concatenate([onehot(take_lo), onehot(take_g), onehot(take_o)], axis=0)
    gate_rows = jnp.zeros((CAP, HD), F32)
    for k in range(heads):
        cols = slice(k * HD, (k + 1) * HD)
        res = dot(take_a, home_a[pl.ds(k * WPH, WPH)].reshape(WPH * MSG, HD))
        dv_ref[:, cols] = res[0:64].astype(BF16)
        dq_ref[:, cols] = res[64:128].astype(BF16)
        res = dot(take_b, home_b[pl.ds(k * WPH, WPH)].reshape(WPH * MSG, HD))
        dk_ref[:, cols] = res[0:64].astype(BF16)
        gated_ref[:, cols] = res[128:160].astype(BF16)
        gate_rows = gate_rows + res[64:128]
    mine_lane = iota((CAP, HD), 1) == (iota((CAP, HD), 0) >> 3)
    gate_grad = jnp.sum(jnp.where(mine_lane, gate_rows, 0.0), axis=1, keepdims=True)
    logit_grad = gate_grad * gate_col * (1.0 - gate_col)
    router_ref[...] = jnp.sum(jnp.where(spots, jnp.broadcast_to(logit_grad, (CAP, TOK)), 0.0), axis=0, keepdims=True)


def body(picked, owner_perm, router_logit, queries, keys, values, out_grad):
    n_tp = lax.axis_size("tp")
    heads = queries.shape[1] // HD
    width = heads * HD
    workers = heads * WPH
    picks = out_grad.shape[0]
    vmem = pl.BlockSpec(memory_space=pltpu.VMEM)
    hbm = pl.BlockSpec(memory_space=pltpu.HBM)
    dma = pltpu.SemaphoreType.DMA
    picked = picked.reshape(1, CAP)
    router_logit = router_logit.reshape(2, TOK // 2)
    start, home_a, home_b = pl.pallas_call(
        functools.partial(kernel, n_tp, heads),
        out_shape=(
            jax.ShapeDtypeStruct((1, 128), I32),
            jax.ShapeDtypeStruct((workers, MSG, HD), BF16),
            jax.ShapeDtypeStruct((workers, MSG, HD), BF16),
        ),
        in_specs=[hbm] * 7,
        out_specs=[vmem, hbm, hbm],
        scratch_shapes=[
            pltpu.VMEM((1, CAP), I32),
            pltpu.VMEM((1, SEQ), I32),
            pltpu.VMEM((2, TOK // 2), BF16),
            pltpu.VMEM((CAP, width), BF16),
            pltpu.VMEM((CAP, width), BF16),
            pltpu.VMEM((CAP, width), BF16),
            pltpu.VMEM((picks, width), BF16),
            pltpu.VMEM((1, 128), I32),
            pltpu.VMEM((SEQ, 1, 128), I32),
            pltpu.VMEM((workers, MSG, HD), BF16),
            pltpu.VMEM((workers, MSG, HD), BF16),
            pltpu.VMEM((SEQ, MSG, HD), BF16),
            pltpu.VMEM((SEQ, MSG, HD), BF16),
            pltpu.VMEM((WPH, CLS, HD), BF16),
            pltpu.VMEM((WPH, CLS, HD), BF16),
            pltpu.VMEM((WPH, 32, HD), BF16),
            pltpu.VMEM((WPH, 32, HD), BF16),
            pltpu.VMEM((3, SEQ * MSG, CLS), BF16),
            pltpu.VMEM((WPH, CLS, CLS), F32),
            pltpu.VMEM((WPH, CLS, CLS), BF16),
            pltpu.VMEM((WPH, CLS, HD), BF16),
            pltpu.VMEM((WPH, CLS, HD), BF16),
            pltpu.VMEM((4, CLS, HD), BF16),
            pltpu.VMEM((4, CLS, HD), BF16),
            pltpu.VMEM((4, CLS, HD), BF16),
            pltpu.VMEM((4, CLS, HD), BF16),
            pltpu.VMEM((WPH, 32, HD), BF16),
            pltpu.VMEM((WPH, 32, HD), BF16),
            pltpu.VMEM((n_tp, 8, CLS), F32),
            pltpu.VMEM((SEQ, MSG, HD), BF16),
            pltpu.VMEM((SEQ, MSG, HD), BF16),
            dma((7,)),
            dma((16,)),
            dma((8,)),
            dma((WPH,)),
            dma((WPH,)),
            dma((4,)),
            dma((4,)),
            dma((4,)),
            dma((4,)),
            dma((2,)),
        ],
        compiler_params=pltpu.CompilerParams(
            collective_id=0, has_side_effects=True, vmem_limit_bytes=60 * 1024 * 1024
        ),
    )(
        picked,
        owner_perm.reshape(1, SEQ),
        router_logit,
        queries,
        keys,
        values,
        out_grad,
    )
    gated, dq, dk, dv, router = pl.pallas_call(
        functools.partial(finish, heads),
        out_shape=(
            jax.ShapeDtypeStruct((picks, width), BF16),
            jax.ShapeDtypeStruct((CAP, width), BF16),
            jax.ShapeDtypeStruct((CAP, width), BF16),
            jax.ShapeDtypeStruct((CAP, width), BF16),
            jax.ShapeDtypeStruct((1, TOK), F32),
        ),
        in_specs=[vmem] * 5,
        out_specs=[vmem] * 5,
        compiler_params=pltpu.CompilerParams(vmem_limit_bytes=60 * 1024 * 1024),
    )(picked, router_logit, start, home_a, home_b)
    return gated, dq, dk, dv, router.reshape(TOK)


def solution(mesh):
    return jax.shard_map(
        body,
        mesh=mesh,
        in_specs=(P("seq"), P(), P("seq"), P("seq", "tp"), P("seq", "tp"), P("seq", "tp"), P("seq", "tp")),
        out_specs=(P("seq", "tp"), P("seq", "tp"), P("seq", "tp"), P("seq", "tp"), P("seq")),
        check_vma=False,
    )
```

time: 85.1 us -> 65.4 us (0.77)
  Pallas kernels: 76.3 us -> 64.6 us
  local copies, waits for them, and re-layouts: 7.9 us -> 0 us
    pallas_call x1, Pallas kernels: 76.3 us -> 62.6 us  [body(): pl.pallas_call(functools.partial(kernel, n_tp, heads), out_shape=(jax.Sha...]
    unnamed x19 -> x0, local copies, waits for them, and re-layouts: 7.89 us -> none
    pallas_call x0 -> x1, Pallas kernels: none -> 2.05 us  [body(): pl.pallas_call(functools.partial(finish, heads), out_shape=(jax.ShapeDtyp...]
where the time goes in v2:
time: 65.4 us; the launch traced here: 65.3 us
  Pallas kernels  64.6 us (99%)
    pallas_call x1, Pallas kernels, body(): pl.pallas_call(functools.partial(kernel, n_tp, heads), out_shape=(jax.Sha...  62.6 us
    pallas_call x1, Pallas kernels, body(): pl.pallas_call(functools.partial(finish, heads), out_shape=(jax.ShapeDtyp...  2.05 us

profile of v2, /device:TPU:1, one launch (start us, length us, event | category | flops | bytes accessed | tf_op | source)
XLA Modules:
  0.0 65.3 jit_solution(16951126517017892899)
XLA Ops:
  0.6 62.6 %shard_map.110 = (s32[1,128]{1,0:T(1,128)}, bf16[48,16,128]{2,1,0:T(8,128)(2,1)}, bf16[48,16,128]{2,1,0:T(8,128)(2,1)}) custom-call(s32[1,64]{1,0:T(1,128)} %bitcast.4, s32[1,64]{1,0:T(1,128)} %bitcast.8, bf16[2,128]{1,0:T(2,128)(2,1)} %bitcast.6, bf16[64,768]{1,0:T(8,128)(2,1)} %q_in.1, bf16[64,768]{1,0:T(8,128)(2,1)} %k_in.1, bf16[64,768]{1,0:T(8,128)(2,1)} %v_in.1, ...), custom_call_target="tpu_custom_call" | custom-call | tf_op jit(solution)/shard_map/pallas_call | solution.py:516
  63.2 2.0 %shard_map.111 = (bf16[32,768]{1,0:T(8,128)(2,1)}, bf16[64,768]{1,0:T(8,128)(2,1)}, bf16[64,768]{1,0:T(8,128)(2,1)}, bf16[64,768]{1,0:T(8,128)(2,1)}, f32[1,256]{1,0:T(1,128)}) custom-call(s32[1,64]{1,0:T(1,128)} %bitcast.5, bf16[2,128]{1,0:T(2,128)(2,1)} %bitcast.7, s32[1,128]{1,0:T(1,128)} %get-tuple-element.13.start_ref, ...), custom_call_target="tpu_custom_call" | custom-call | tf_op jit(solution)/shard_map/pallas_call | solution.py:580

commit v3 on v2

--- a/solution.py
+++ b/solution.py
@@ -15,6 +15,7 @@
 CLS = 256
 MSG = 16
 SCALE = HD ** -0.5
+SCALE_LOG2 = SCALE * 1.4426950408889634
 MESH = pl.DeviceIdType.MESH
 BF16, F32, I32 = jnp.bfloat16, jnp.float32, jnp.int32
 
@@ -70,7 +71,9 @@
     v_in,
     d_in,
     start_ref,
-    home_a,
+    gate_ref,
+    home_c_out,
+    home_q,
     home_b,
     picked_ref,
     perm_ref,
@@ -81,15 +84,18 @@
     d_ref,
     cnt_out,
     cnt,
-    msg_a,
+    msg_k,
+    msg_v,
     msg_b,
-    rows_a,
+    rows_k,
+    rows_v,
     rows_b,
     k_all,
     v_all,
     dsend,
     dcls,
     put,
+    put_e,
     sbuf,
     pbuf,
     part_k,
@@ -101,8 +107,10 @@
     gsend,
     gchk,
     gg,
-    back_a,
+    back_q,
+    back_c,
     back_b,
+    home_c,
     in_sem,
     send_sem,
     recv_sem,
@@ -174,60 +182,64 @@
     start = jnp.sum(jnp.where(iota((SEQ, 128), 0) < me, counts, 0), axis=0, keepdims=True)
     start_ref[...] = start
 
+    n_half = iota((WPH * 8, CAP), 0)
+    turn_half = ((n_half >> 3) - start[:, :CAP]) & 7
+    pick_half = onehot(iota((WPH * 8, CAP), 1) == 8 * (n_half & 7) + turn_half)
     n_out = iota((WPH * MSG, 128), 0)
     t_out = n_out & 15
     turn = ((n_out >> 4) - start) & 7
     src = iota((WPH * MSG, 128), 1)
-    pick_a = onehot(src == 8 * t_out + turn)
     b_from = jnp.where(t_out < 8, 8 * t_out + turn, jnp.where(t_out < 12, CAP + 4 * (n_out >> 4) + t_out - 8, -1))
     pick_b = onehot(src == b_from)
     src64 = iota((WPH * MSG, CAP), 1)
     pick_logit = onehot((t_out[:, :CAP] == 12) & ((src64 & 7) == turn[:, :CAP]))
 
-    def send_rows(msg, rows, sem):
+    def send_rows(msg, rows, sem, recv):
         def send_one(n, carry):
             w = lax.rem(n + me, workers)
             dst = place_of(lax.div(w, WPH), lax.rem(w, WPH))
 
             @pl.when(dst != me)
             def _():
-                remote(msg.at[w], rows.at[me], send_sem.at[sem], recv_sem.at[sem], {"seq": dst}).start()
+                remote(msg.at[w], rows.at[me], send_sem.at[sem], recv_sem.at[recv], {"seq": dst}).start()
 
             return carry
 
         lax.fori_loop(0, workers, send_one, 0)
 
-    for k in range(heads):
-        cols = slice(k * HD, (k + 1) * HD)
-        both = dot(pick_a, jnp.concatenate([k_ref[:, cols], q_ref[:, cols]], axis=0))
-        msg_a[pl.ds(k * WPH, WPH)] = both.astype(BF16).reshape(WPH, MSG, HD)
-    send_rows(msg_a, rows_a, 1)
+    for ref, msg, rows, sem, recv in ((k_ref, msg_k, rows_k, 1, 1), (v_ref, msg_v, rows_v, 16, 8)):
+        turned = dot(pick_half, ref[...]).astype(BF16)
+        for k in range(heads):
+            msg[pl.ds(k * WPH, WPH)] = turned[:, k * HD : (k + 1) * HD].reshape(WPH, 8, HD)
+        send_rows(msg, rows, sem, recv)
     logit_rows = dot(pick_logit, spread)
     for k in range(heads):
         cols = slice(k * HD, (k + 1) * HD)
-        both = dot(pick_b, jnp.concatenate([v_ref[:, cols], d_ref[:, cols], fill], axis=0)) + logit_rows
+        both = dot(pick_b, jnp.concatenate([q_ref[:, cols], d_ref[:, cols], fill], axis=0)) + logit_rows
         msg_b[pl.ds(k * WPH, WPH)] = both.astype(BF16).reshape(WPH, MSG, HD)
-    send_rows(msg_b, rows_b, 2)
+    send_rows(msg_b, rows_b, 2, 2)
+    left = []
+
+    def gone(src, sem):
+        left.append((src, sem))
+
+    def done():
+        for src, sem in left:
+            remote(src, src, send_sem.at[sem], recv_sem.at[0], sibling).wait_send()
+
+    def came(ref, sem):
+        remote(ref, ref, send_sem.at[0], sem, sibling).wait_recv()
 
     @pl.when(is_worker)
     def _():
-        left = []
-
-        def gone(src, sem):
-            left.append((src, sem))
-
-        def done():
-            for src, sem in left:
-                remote(src, src, send_sem.at[sem], recv_sem.at[0], sibling).wait_send()
-
-        def came(ref, sem):
-            remote(ref, ref, send_sem.at[0], sem, sibling).wait_recv()
-
-        own_a = pltpu.make_async_copy(msg_a.at[slot], rows_a.at[me], loc_sem.at[0])
-        own_a.start()
+        own_k = pltpu.make_async_copy(msg_k.at[slot], rows_k.at[me], loc_sem.at[0])
+        own_k.start()
+        own_v = pltpu.make_async_copy(msg_v.at[slot], rows_v.at[me], loc_sem.at[3])
+        own_v.start()
         own_b = pltpu.make_async_copy(msg_b.at[slot], rows_b.at[me], loc_sem.at[1])
         own_b.start()
-        gone(msg_a.at[pl.ds(0, workers - 1)], 1)
+        gone(msg_k.at[pl.ds(0, workers - 1)], 1)
+        gone(msg_v.at[pl.ds(0, workers - 1)], 16)
         gone(msg_b.at[pl.ds(0, workers - 1)], 2)
 
         def peer(n, flip):
@@ -254,17 +266,24 @@
         p_n = ((start_n - cls + 7) >> 3) + (t_n & 7)
         live_n = p_n < ((end_n - cls + 7) >> 3)
         lo_at = jnp.where(live_n & (t_n < 8), p_n, -1)
-        hi_at = jnp.where(live_n & (t_n >= 8), p_n, -1)
         p_sub = iota((CLS, SEQ * MSG), 0)
         take_lo = onehot(p_sub == lo_at)
-        take_hi = onehot(p_sub == hi_at)
-
-        came(rows_a.at[pl.ds(0, SEQ - 1)], recv_sem.at[1])
-        own_a.wait()
-        a_rows = rows_a[...].reshape(SEQ * MSG, HD)
-        k_all[cls] = dot(take_lo, a_rows).astype(BF16)
+
+        n_eight = iota((SEQ, SEQ * 8), 1)
+        start_e = jnp.sum(jnp.where(at_h[:, : SEQ * 8] < (n_eight >> 3), below[:, : SEQ * 8], 0), axis=0, keepdims=True)
+        end_e = jnp.sum(jnp.where(at_h[:, : SEQ * 8] <= (n_eight >> 3), below[:, : SEQ * 8], 0), axis=0, keepdims=True)
+        p_e = ((start_e - cls + 7) >> 3) + (n_eight[0:1] & 7)
+        e_at = jnp.where(p_e < ((end_e - cls + 7) >> 3), p_e, -1)
+        take_eight = onehot(p_sub[:, : SEQ * 8] == e_at)
+
+        came(rows_k.at[pl.ds(0, SEQ - 1)], recv_sem.at[1])
+        own_k.wait()
+        k_all[cls] = dot(take_eight, rows_k[...].reshape(SEQ * 8, HD)).astype(BF16)
         send_all(k_all, k_sem, 3)
-        q = dot(take_hi, a_rows).astype(BF16)
+        came(rows_v.at[pl.ds(0, SEQ - 1)], recv_sem.at[8])
+        own_v.wait()
+        v_all[cls] = dot(take_eight, rows_v[...].reshape(SEQ * 8, HD)).astype(BF16)
+        send_all(v_all, v_sem, 4)
 
         m_sub = iota((CLS, SEQ), 0)
         residue_m = 8 * (m_sub & 7) + (m_sub >> 5)
@@ -289,25 +308,29 @@
         perm_o = jnp.broadcast_to(perm_ref[...], (SEQ, SEQ))
         res_o = jnp.sum(jnp.where(perm_o == iota((SEQ, SEQ), 0), iota((SEQ, SEQ), 1), 0), axis=1, keepdims=True)
         three = jnp.concatenate([base, after, jnp.broadcast_to(res_o, (SEQ, 128))], axis=1).astype(F32).astype(BF16)
-        wide = dot(rep, three).astype(I32)
+        wide = dot(rep, three[:, :256]).astype(I32)
         t_col = iota((SEQ * MSG, 128), 0) & 15
         p_col = wide[:, :128] + (t_col & 7)
         live_col = p_col < wide[:, 128:256]
-        res_col = wide[:, 256:]
         lo_to = jnp.where(live_col & (t_col < 8), p_col, -1)
         hi_to = jnp.where(live_col & (t_col >= 8), p_col, -1)
-        o_to = jnp.where((t_col >= 8) & (t_col < 12), 32 * (res_col & 7) + 8 * (t_col - 8) + (res_col >> 3), -1)
         p_at = iota((SEQ * MSG, CLS), 1)
         put[0] = onehot(p_at == jnp.concatenate([lo_to, lo_to], axis=1))
         put[1] = onehot(p_at == jnp.concatenate([hi_to, hi_to], axis=1))
-        put[2] = onehot(p_at == jnp.concatenate([o_to, o_to], axis=1))
-        put_g = onehot(iota((SEQ * MSG, SEQ), 0) == MSG * iota((SEQ * MSG, SEQ), 1) + 12)
+        rep_e = onehot((iota((SEQ * 8, SEQ), 0) >> 3) == iota((SEQ * 8, SEQ), 1))
+        wide_e = dot(rep_e, three).astype(I32)
+        t_e = iota((SEQ * 8, 128), 0) & 7
+        e_col = wide_e[:, :128] + t_e
+        e_to = jnp.where(e_col < wide_e[:, 128:256], e_col, -1)
+        res_e = wide_e[:, 256:]
+        o_to = jnp.where(t_e < 4, 32 * (res_e & 7) + 8 * t_e + (res_e >> 3), -1)
+        put_e[0] = onehot(p_at[: SEQ * 8] == jnp.concatenate([e_to, e_to], axis=1))
+        put_e[1] = onehot(p_at[: SEQ * 8] == jnp.concatenate([o_to, o_to], axis=1))
+        put_g = onehot(iota((SEQ * 8, SEQ), 0) == 8 * iota((SEQ * 8, SEQ), 1) + 4)
 
         came(rows_b.at[pl.ds(0, SEQ - 1)], recv_sem.at[2])
         own_b.wait()
         b_rows = rows_b[...].reshape(SEQ * MSG, HD)
-        v_all[cls] = dot(take_lo, b_rows).astype(BF16)
-        send_all(v_all, v_sem, 4)
         dsend[...] = dot(take_d, b_rows).astype(BF16).reshape(WPH, 32, HD)
 
         def send_d(n, carry):
@@ -318,6 +341,7 @@
         lax.fori_loop(1, WPH, send_d, 0)
         dcls[cls] = dsend[cls]
         gone(dsend.at[pl.ds(0, WPH - 1)], 6)
+        q = dot(take_lo, b_rows).astype(BF16)
         for n in (1, 3):
             pass_on(k_all, k_sem, 5, n)
         logit_h = dot(take_l, b_rows).astype(BF16)
@@ -325,7 +349,7 @@
         gate = 1.0 / (1.0 + jnp.exp(-logit_p))
 
         top = jnp.full((1, CLS), -jnp.inf, F32)
-        k_sub, q_lane = iota((CLS, CLS), 0), iota((CLS, CLS), 1)
+        ahead = iota((CLS, CLS), 1) - iota((CLS, CLS), 0)
         order = ((0, 0), (0, 1), (1, 0), (3, 0), (1, 1), (3, 1), (2, 0), (2, 1))
         for n, flip in order:
             other = peer(n, flip)
@@ -334,26 +358,23 @@
             if flip:
                 came(k_all.at[other], k_sem.at[other])
             later = jnp.where(other > cls, 1, 0)
-            s = dot_nt(k_all[other], q) * SCALE
-            s = jnp.where(k_sub + later <= q_lane, s, -1e30)
+            s = jnp.where(ahead >= later, dot_nt(k_all[other], q), -1e30)
             sbuf[2 * n + flip] = s
             top = jnp.maximum(top, jnp.max(s, axis=0, keepdims=True))
         gone(k_all.at[pl.ds(0, 3)], 5)
+        for n in (1, 3):
+            pass_on(v_all, v_sem, 7, n)
         total = jnp.zeros((1, CLS), F32)
         for n in range(WPH):
-            e = jnp.exp(sbuf[n] - top)
-            sbuf[n] = e
+            e = jnp.exp2((sbuf[n] - top) * SCALE_LOG2)
+            pbuf[n] = e.astype(BF16)
             total = total + jnp.sum(e, axis=0, keepdims=True)
         inv = 1.0 / total
-        for n in range(WPH):
-            w = sbuf[n] * inv
-            sbuf[n] = w
-            pbuf[n] = w.astype(BF16)
 
         came(dcls.at[pl.ds(0, WPH - 1)], recv_sem.at[3])
         dy_t = dcls[...].reshape(CLS, HD).astype(F32).T
         dor_t = (dy_t * gate).astype(BF16).astype(F32)
-        dor = dor_t.T.astype(BF16)
+        dor = (dor_t * inv).T.astype(BF16)
 
         def to_sibling(grads, part, pre, sems, sem, n):
             part[2 * n + 1] = grads.astype(BF16)
@@ -379,11 +400,6 @@
         for n in far_first:
             to_sibling(dot(pbuf[2 * n + 1], dor), part_v, pre_v, pre_v_sem, 9, n)
         gone(part_v.at[pl.ds(0, 4)], 9)
-        for n in (1, 3):
-            pass_on(v_all, v_sem, 7, n)
-        for n in far_first:
-            mine_v = to_class(dot(pbuf[2 * n], dor), part_v, pre_v, pre_v_sem, sum_v, sum_v_sem, 10, n)
-        gone(part_v.at[pl.ds(0, 3)], 10)
         pass_on(v_all, v_sem, 7, 2)
         gone(v_all.at[pl.ds(0, 3)], 7)
         out_t = jnp.zeros((HD, CLS), F32)
@@ -392,10 +408,10 @@
             if flip:
                 came(v_all.at[other], v_sem.at[other])
             out_t = out_t + dot_tn(v_all[other], pbuf[2 * n + flip])
-        delta = jnp.sum(dor_t * out_t, axis=0, keepdims=True)
+        out_t = out_t * inv
+        delta = jnp.sum(dor_t * out_t, axis=0, keepdims=True) * inv
         gate_grad = jnp.sum(dy_t * out_t, axis=0, keepdims=True)
         gsend[...] = (out_t * gate).T.astype(BF16).reshape(WPH, 32, HD)
-        gg[tp] = jnp.broadcast_to(gate_grad, (8, CLS))
 
         def send_gated(n, carry):
             to = lax.rem(cls + n, WPH)
@@ -405,72 +421,94 @@
         lax.fori_loop(1, WPH, send_gated, 0)
         gchk[cls] = gsend[cls]
         gone(gsend.at[pl.ds(0, WPH - 1)], 8)
-        if n_tp > 1:
-            for n in range(1, n_tp):
-                remote(gg.at[tp], gg.at[tp], send_sem.at[13], recv_sem.at[5], {"tp": lax.rem(tp + n, n_tp)}).start()
-            gone(gg.at[pl.ds(0, n_tp - 1)], 13)
-
+        for n in far_first:
+            mine_v = to_class(dot(pbuf[2 * n], dor), part_v, pre_v, pre_v_sem, sum_v, sum_v_sem, 10, n)
+        gone(part_v.at[pl.ds(0, 3)], 10)
         dq_t = jnp.zeros((HD, CLS), F32)
         for flip in (1, 0):
             for n in far_first:
                 other = peer(n, flip)
                 dp = dot_nt(v_all[other], dor)
-                ds = (sbuf[2 * n + flip] * (dp - delta)).astype(BF16)
+                ds = (pbuf[2 * n + flip].astype(F32) * (dp - delta)).astype(BF16)
                 dq_t = dq_t + dot_tn(k_all[other], ds)
-                grads = dot(ds, q) * SCALE
                 if flip:
-                    to_sibling(grads, part_k, pre_k, pre_k_sem, 11, n)
+                    to_sibling(dot(ds, q) * SCALE, part_k, pre_k, pre_k_sem, 11, n)
                 else:
-                    mine_k = to_class(grads, part_k, pre_k, pre_k_sem, sum_k, sum_k_sem, 12, n)
+                    pbuf[2 * n] = ds
+        for n in far_first:
+            mine_k = to_class(dot(pbuf[2 * n], q) * SCALE, part_k, pre_k, pre_k_sem, sum_k, sum_k_sem, 12, n)
         gone(part_k.at[pl.ds(0, 4)], 11)
         gone(part_k.at[pl.ds(0, 3)], 12)
 
-        def send_back(back, home, sem):
+        def send_back(back, home, sem, recv, own):
             def send_one(n, carry):
                 to = lax.rem(me + n, SEQ)
-                remote(back.at[to], home.at[slot], send_sem.at[sem], recv_sem.at[sem - 8], {"seq": to}).start()
+                remote(back.at[to], home.at[slot], send_sem.at[sem], recv_sem.at[recv], {"seq": to}).start()
                 return carry
 
             lax.fori_loop(1, SEQ, send_one, 0)
             gone(back.at[pl.ds(0, SEQ - 1)], sem)
+            mine = pltpu.make_async_copy(back.at[me], home.at[slot], loc_sem.at[own])
+            mine.start()
+            return mine
 
         dqc = (dq_t * SCALE).T.astype(BF16)
-        mine_v = collect(mine_v, sum_v, sum_v_sem)
-        full = dot(put[0], mine_v) + dot(put[1], dqc)
-        back_a[...] = full.astype(BF16).reshape(SEQ, MSG, HD)
-        send_back(back_a, home_a, 14)
-        own_a = pltpu.make_async_copy(back_a.at[me], home_a.at[slot], loc_sem.at[0])
-        own_a.start()
-        if n_tp > 1:
-            came(gg.at[pl.ds(0, n_tp - 1)], recv_sem.at[5])
-        gate_sum = jnp.sum(gg[...], axis=0)[0:1]
-        gg_home = dot_nt(jnp.where(of_home, gate_sum, 0.0).astype(BF16), lanes).astype(BF16)
+        back_q[...] = dot(put_e[0], dqc).astype(BF16).reshape(SEQ, 8, HD)
+        own_q = send_back(back_q, home_q, 14, 6, 1)
+        gg_home = dot_nt(jnp.where(of_home, gate_grad, 0.0).astype(BF16), lanes).astype(BF16)
         came(gchk.at[pl.ds(0, WPH - 1)], recv_sem.at[4])
-        rest = dot(put_g, gg_home) + dot(put[2], gchk[...].reshape(CLS, HD))
-        mine_k = collect(mine_k, sum_k, sum_k_sem)
-        full = dot(put[0], mine_k) + rest
+        full = dot(put_g, gg_home) + dot(put_e[1], gchk[...].reshape(CLS, HD))
+        back_c[...] = full.astype(BF16).reshape(SEQ, 8, HD)
+        own_c = send_back(back_c, home_c, 17, 9, 3)
+        rest = dot(put[1], collect(mine_v, sum_v, sum_v_sem))
+        full = dot(put[0], collect(mine_k, sum_k, sum_k_sem)) + rest
         back_b[...] = full.astype(BF16).reshape(SEQ, MSG, HD)
-        send_back(back_b, home_b, 15)
-        own_b = pltpu.make_async_copy(back_b.at[me], home_b.at[slot], loc_sem.at[1])
-        own_b.start()
-        done()
-        own_a.wait()
+        own_b = send_back(back_b, home_b, 15, 7, 0)
+        own_q.wait()
+        own_c.wait()
         own_b.wait()
-        came(home_a.at[pl.ds(0, workers - 1)], recv_sem.at[6])
-        came(home_b.at[pl.ds(0, workers - 1)], recv_sem.at[7])
+        came(home_c.at[pl.ds(0, workers - 1)], recv_sem.at[9])
 
     @pl.when(jnp.logical_not(is_worker))
     def _():
-        remote(msg_a, msg_a, send_sem.at[1], recv_sem.at[1], sibling).wait_send()
+        came(home_c, recv_sem.at[9])
+
+    keep_c = pltpu.make_async_copy(home_c, home_c_out, loc_sem.at[2])
+    keep_c.start()
+    gate_rows = jnp.zeros((CAP, HD), F32)
+    take_g = onehot((iota((CAP, 128), 1) == 8 * ((start + iota((CAP, 128), 0)) & 7) + 4)[:, :CAP])
+    for k in range(heads):
+        gate_rows = gate_rows + dot(take_g, home_c[pl.ds(k * WPH, WPH)].reshape(WPH * 8, HD))
+    mine_lane = iota((CAP, HD), 1) == (iota((CAP, HD), 0) >> 3)
+    gate_grad = jnp.sum(jnp.where(mine_lane, gate_rows, 0.0), axis=1, keepdims=True)
+    gg[tp] = jnp.broadcast_to(gate_grad, (CAP, 128))
+    for n in range(1, n_tp):
+        remote(gg.at[tp], gg.at[tp], send_sem.at[13], recv_sem.at[5], {"tp": lax.rem(tp + n, n_tp)}).start()
+
+    @pl.when(is_worker)
+    def _():
+        done()
+        came(home_q.at[pl.ds(0, workers - 1)], recv_sem.at[6])
+        came(home_b.at[pl.ds(0, workers - 1)], recv_sem.at[7])
+
+    @pl.when(jnp.logical_not(is_worker))
+    def _():
+        remote(msg_k, msg_k, send_sem.at[1], recv_sem.at[1], sibling).wait_send()
+        remote(msg_v, msg_v, send_sem.at[16], recv_sem.at[8], sibling).wait_send()
         remote(msg_b, msg_b, send_sem.at[2], recv_sem.at[2], sibling).wait_send()
-        remote(home_a, home_a, send_sem.at[14], recv_sem.at[6], sibling).wait_recv()
-        remote(home_b, home_b, send_sem.at[15], recv_sem.at[7], sibling).wait_recv()
-
+        came(home_q, recv_sem.at[6])
+        came(home_b, recv_sem.at[7])
+
+    if n_tp > 1:
+        others = gg.at[pl.ds(0, n_tp - 1)]
+        remote(others, others, send_sem.at[13], recv_sem.at[5], sibling).wait()
+    gate_ref[...] = jnp.sum(gg[...], axis=0)
+    keep_c.wait()
     remote(counted, counted, send_sem.at[0], recv_sem.at[0], sibling).wait_send()
 
 
 def finish(
-    heads, picked_ref, logit_ref, start_ref, home_a, home_b, gated_ref, dq_ref, dk_ref, dv_ref, router_ref
+    heads, picked_ref, logit_ref, start_ref, gate_ref, home_c, home_q, home_b, gated_ref, dq_ref, dk_ref, dv_ref, router_ref
 ):
     me = lax.axis_index("seq")
     start = start_ref[...]
@@ -481,23 +519,17 @@
     from_cls = MSG * ((start + j) & 7)
     lo = from_cls + (j >> 3)
     take_lo = col == lo
-    take_hi = col == lo + 8
-    take_g = col == from_cls + 12
-    take_o = (col == MSG * (j >> 2) + 8 + (j & 3)) & (j < 32)
-    take_a = jnp.concatenate([onehot(take_lo), onehot(take_hi)], axis=0)
-    take_b = jnp.concatenate([onehot(take_lo), onehot(take_g), onehot(take_o)], axis=0)
-    gate_rows = jnp.zeros((CAP, HD), F32)
+    take_e = onehot((col == 8 * ((start + j) & 7) + (j >> 3))[:, :CAP])
+    take_o = onehot(((col == 8 * (j >> 2) + (j & 3)) & (j < 32))[:32, :CAP])
+    take_b = jnp.concatenate([onehot(take_lo), onehot(col == lo + 8)], axis=0)
     for k in range(heads):
         cols = slice(k * HD, (k + 1) * HD)
-        res = dot(take_a, home_a[pl.ds(k * WPH, WPH)].reshape(WPH * MSG, HD))
-        dv_ref[:, cols] = res[0:64].astype(BF16)
-        dq_ref[:, cols] = res[64:128].astype(BF16)
+        dq_ref[:, cols] = dot(take_e, home_q[pl.ds(k * WPH, WPH)].reshape(WPH * 8, HD)).astype(BF16)
+        gated_ref[:, cols] = dot(take_o, home_c[pl.ds(k * WPH, WPH)].reshape(WPH * 8, HD)).astype(BF16)
         res = dot(take_b, home_b[pl.ds(k * WPH, WPH)].reshape(WPH * MSG, HD))
         dk_ref[:, cols] = res[0:64].astype(BF16)
-        gated_ref[:, cols] = res[128:160].astype(BF16)
-        gate_rows = gate_rows + res[64:128]
-    mine_lane = iota((CAP, HD), 1) == (iota((CAP, HD), 0) >> 3)
-    gate_grad = jnp.sum(jnp.where(mine_lane, gate_rows, 0.0), axis=1, keepdims=True)
+        dv_ref[:, cols] = res[64:128].astype(BF16)
+    gate_grad = gate_ref[...][:, 0:1]
     logit_grad = gate_grad * gate_col * (1.0 - gate_col)
     router_ref[...] = jnp.sum(jnp.where(spots, jnp.broadcast_to(logit_grad, (CAP, TOK)), 0.0), axis=0, keepdims=True)
 
@@ -513,15 +545,17 @@
     dma = pltpu.SemaphoreType.DMA
     picked = picked.reshape(1, CAP)
     router_logit = router_logit.reshape(2, TOK // 2)
-    start, home_a, home_b = pl.pallas_call(
+    start, gate_grad, home_c, home_q, home_b = pl.pallas_call(
         functools.partial(kernel, n_tp, heads),
         out_shape=(
             jax.ShapeDtypeStruct((1, 128), I32),
-            jax.ShapeDtypeStruct((workers, MSG, HD), BF16),
+            jax.ShapeDtypeStruct((CAP, 128), F32),
+            jax.ShapeDtypeStruct((workers, 8, HD), BF16),
+            jax.ShapeDtypeStruct((workers, 8, HD), BF16),
             jax.ShapeDtypeStruct((workers, MSG, HD), BF16),
         ),
         in_specs=[hbm] * 7,
-        out_specs=[vmem, hbm, hbm],
+        out_specs=[vmem, vmem, hbm, hbm, hbm],
         scratch_shapes=[
             pltpu.VMEM((1, CAP), I32),
             pltpu.VMEM((1, SEQ), I32),
@@ -532,15 +566,18 @@
             pltpu.VMEM((picks, width), BF16),
             pltpu.VMEM((1, 128), I32),
             pltpu.VMEM((SEQ, 1, 128), I32),
+            pltpu.VMEM((workers, 8, HD), BF16),
+            pltpu.VMEM((workers, 8, HD), BF16),
             pltpu.VMEM((workers, MSG, HD), BF16),
-            pltpu.VMEM((workers, MSG, HD), BF16),
-            pltpu.VMEM((SEQ, MSG, HD), BF16),
+            pltpu.VMEM((SEQ, 8, HD), BF16),
+            pltpu.VMEM((SEQ, 8, HD), BF16),
             pltpu.VMEM((SEQ, MSG, HD), BF16),
             pltpu.VMEM((WPH, CLS, HD), BF16),
             pltpu.VMEM((WPH, CLS, HD), BF16),
             pltpu.VMEM((WPH, 32, HD), BF16),
             pltpu.VMEM((WPH, 32, HD), BF16),
-            pltpu.VMEM((3, SEQ * MSG, CLS), BF16),
+            pltpu.VMEM((2, SEQ * MSG, CLS), BF16),
+            pltpu.VMEM((2, SEQ * 8, CLS), BF16),
             pltpu.VMEM((WPH, CLS, CLS), F32),
             pltpu.VMEM((WPH, CLS, CLS), BF16),
             pltpu.VMEM((WPH, CLS, HD), BF16),
@@ -551,19 +588,21 @@
             pltpu.VMEM((4, CLS, HD), BF16),
             pltpu.VMEM((WPH, 32, HD), BF16),
             pltpu.VMEM((WPH, 32, HD), BF16),
-            pltpu.VMEM((n_tp, 8, CLS), F32),
+            pltpu.VMEM((n_tp, CAP, 128), F32),
+            pltpu.VMEM((SEQ, 8, HD), BF16),
+            pltpu.VMEM((SEQ, 8, HD), BF16),
             pltpu.VMEM((SEQ, MSG, HD), BF16),
-            pltpu.VMEM((SEQ, MSG, HD), BF16),
+            pltpu.VMEM((workers, 8, HD), BF16),
             dma((7,)),
-            dma((16,)),
-            dma((8,)),
+            dma((18,)),
+            dma((10,)),
             dma((WPH,)),
             dma((WPH,)),
             dma((4,)),
             dma((4,)),
             dma((4,)),
             dma((4,)),
-            dma((2,)),
+            dma((4,)),
         ],
         compiler_params=pltpu.CompilerParams(
             collective_id=0, has_side_effects=True, vmem_limit_bytes=60 * 1024 * 1024
@@ -586,10 +625,10 @@
             jax.ShapeDtypeStruct((CAP, width), BF16),
             jax.ShapeDtypeStruct((1, TOK), F32),
         ),
-        in_specs=[vmem] * 5,
+        in_specs=[vmem] * 7,
         out_specs=[vmem] * 5,
         compiler_params=pltpu.CompilerParams(vmem_limit_bytes=60 * 1024 * 1024),
-    )(picked, router_logit, start, home_a, home_b)
+    )(picked, router_logit, start, gate_grad, home_c, home_q, home_b)
     return gated, dq, dk, dv, router.reshape(TOK)
 
 

time: 65.4 us -> 63.5 us (0.971)
  Pallas kernels: 64.6 us -> 62.7 us
    pallas_call x1, Pallas kernels: 62.6 us -> 60.7 us  [body(): pl.pallas_call(functools.partial(kernel, n_tp, heads), out_shape=(jax.Sha...]
where the time goes in v3:
time: 63.5 us; the launch traced here: 63.4 us
  Pallas kernels  62.7 us (99%)
  between operations  0.64 us (1%)
    pallas_call x1, Pallas kernels, body(): pl.pallas_call(functools.partial(kernel, n_tp, heads), out_shape=(jax.Sha...  60.7 us
    pallas_call x1, Pallas kernels, body(): pl.pallas_call(functools.partial(finish, heads), out_shape=(jax.ShapeDtyp...  2.06 us

profile of v3, /device:TPU:1, one launch (start us, length us, event | category | flops | bytes accessed | tf_op | source)
XLA Modules:
  0.0 63.4 jit_solution(5202615054291989971)
XLA Ops:
  0.6 60.7 %shard_map.110 = (s32[1,128]{1,0:T(1,128)}, f32[64,128]{1,0:T(8,128)}, bf16[48,8,128]{2,1,0:T(8,128)(2,1)}, bf16[48,8,128]{2,1,0:T(8,128)(2,1)}, bf16[48,16,128]{2,1,0:T(8,128)(2,1)}) custom-call(s32[1,64]{1,0:T(1,128)} %bitcast.4, s32[1,64]{1,0:T(1,128)} %bitcast.8, bf16[2,128]{1,0:T(2,128)(2,1)} %bitcast.6, bf16[64,768]{1,0:T(8,128)(2,1)} %q_in.1, ...), custom_call_target="tpu_custom_call" | custom-call | tf_op jit(solution)/shard_map/pallas_call | solution.py:548
  61.3 2.1 %shard_map.111 = (bf16[32,768]{1,0:T(8,128)(2,1)}, bf16[64,768]{1,0:T(8,128)(2,1)}, bf16[64,768]{1,0:T(8,128)(2,1)}, bf16[64,768]{1,0:T(8,128)(2,1)}, f32[1,256]{1,0:T(1,128)}) custom-call(s32[1,64]{1,0:T(1,128)} %bitcast.5, bf16[2,128]{1,0:T(2,128)(2,1)} %bitcast.7, s32[1,128]{1,0:T(1,128)} %get-tuple-element.15.start_ref, ...), custom_call_target="tpu_custom_call" | custom-call | tf_op jit(solution)/shard_map/pallas_call | solution.py:619

commit v4 on v3

--- a/solution.py
+++ b/solution.py
@@ -152,7 +152,7 @@
         pl.semaphore_signal(barrier, inc=1, device_id={"seq": lax.rem(me + n, SEQ)}, device_id_type=MESH)
         return carry
 
-    lax.fori_loop(1, SEQ, greet, 0)
+    lax.fori_loop(1, SEQ, greet, 0, unroll=7)
     for n in range(1, n_tp):
         pl.semaphore_signal(barrier, inc=1, device_id={"tp": lax.rem(tp + n, n_tp)}, device_id_type=MESH)
 
@@ -166,7 +166,7 @@
         remote(cnt_out, cnt.at[me], send_sem.at[0], recv_sem.at[0], {"seq": lax.rem(me + n, SEQ)}).start()
         return carry
 
-    lax.fori_loop(1, SEQ, send_count, 0)
+    lax.fori_loop(1, SEQ, send_count, 0, unroll=7)
     cnt[me] = cnt_out[...]
 
     for load in loads[1:]:
@@ -205,7 +205,7 @@
 
             return carry
 
-        lax.fori_loop(0, workers, send_one, 0)
+        lax.fori_loop(0, workers, send_one, 0, unroll=6)
 
     for ref, msg, rows, sem, recv in ((k_ref, msg_k, rows_k, 1, 1), (v_ref, msg_v, rows_v, 16, 8)):
         turned = dot(pick_half, ref[...]).astype(BF16)
@@ -401,6 +401,9 @@
             to_sibling(dot(pbuf[2 * n + 1], dor), part_v, pre_v, pre_v_sem, 9, n)
         gone(part_v.at[pl.ds(0, 4)], 9)
         pass_on(v_all, v_sem, 7, 2)
+        for n in far_first:
+            mine_v = to_class(dot(pbuf[2 * n], dor), part_v, pre_v, pre_v_sem, sum_v, sum_v_sem, 10, n)
+        gone(part_v.at[pl.ds(0, 3)], 10)
         gone(v_all.at[pl.ds(0, 3)], 7)
         out_t = jnp.zeros((HD, CLS), F32)
         for n, flip in order:
@@ -421,9 +424,6 @@
         lax.fori_loop(1, WPH, send_gated, 0)
         gchk[cls] = gsend[cls]
         gone(gsend.at[pl.ds(0, WPH - 1)], 8)
-        for n in far_first:
-            mine_v = to_class(dot(pbuf[2 * n], dor), part_v, pre_v, pre_v_sem, sum_v, sum_v_sem, 10, n)
-        gone(part_v.at[pl.ds(0, 3)], 10)
         dq_t = jnp.zeros((HD, CLS), F32)
         for flip in (1, 0):
             for n in far_first:
@@ -446,7 +446,7 @@
                 remote(back.at[to], home.at[slot], send_sem.at[sem], recv_sem.at[recv], {"seq": to}).start()
                 return carry
 
-            lax.fori_loop(1, SEQ, send_one, 0)
+            lax.fori_loop(1, SEQ, send_one, 0, unroll=7)
             gone(back.at[pl.ds(0, SEQ - 1)], sem)
             mine = pltpu.make_async_copy(back.at[me], home.at[slot], loc_sem.at[own])
             mine.start()

time: 63.5 us -> 62.5 us (0.984)
  Pallas kernels: 62.7 us -> 61.8 us
    pallas_call x1, Pallas kernels: 60.7 us -> 59.7 us  [body(): pl.pallas_call(functools.partial(kernel, n_tp, heads), out_shape=(jax.Sha...]
where the time goes in v4:
time: 62.5 us; the launch traced here: 62.4 us
  Pallas kernels  61.8 us (99%)
  between operations  0.64 us (1%)
    pallas_call x1, Pallas kernels, body(): pl.pallas_call(functools.partial(kernel, n_tp, heads), out_shape=(jax.Sha...  59.7 us
    pallas_call x1, Pallas kernels, body(): pl.pallas_call(functools.partial(finish, heads), out_shape=(jax.ShapeDtyp...  2.06 us

profile of v4, /device:TPU:1, one launch (start us, length us, event | category | flops | bytes accessed | tf_op | source)
XLA Modules:
  0.0 62.4 jit_solution(8182399741835277622)
XLA Ops:
  0.6 59.7 %shard_map.110 = (s32[1,128]{1,0:T(1,128)}, f32[64,128]{1,0:T(8,128)}, bf16[48,8,128]{2,1,0:T(8,128)(2,1)}, bf16[48,8,128]{2,1,0:T(8,128)(2,1)}, bf16[48,16,128]{2,1,0:T(8,128)(2,1)}) custom-call(s32[1,64]{1,0:T(1,128)} %bitcast.4, s32[1,64]{1,0:T(1,128)} %bitcast.8, bf16[2,128]{1,0:T(2,128)(2,1)} %bitcast.6, bf16[64,768]{1,0:T(8,128)(2,1)} %q_in.1, ...), custom_call_target="tpu_custom_call" | custom-call | tf_op jit(solution)/shard_map/pallas_call | solution.py:548
  60.4 2.1 %shard_map.111 = (bf16[32,768]{1,0:T(8,128)(2,1)}, bf16[64,768]{1,0:T(8,128)(2,1)}, bf16[64,768]{1,0:T(8,128)(2,1)}, bf16[64,768]{1,0:T(8,128)(2,1)}, f32[1,256]{1,0:T(1,128)}) custom-call(s32[1,64]{1,0:T(1,128)} %bitcast.5, bf16[2,128]{1,0:T(2,128)(2,1)} %bitcast.7, s32[1,128]{1,0:T(1,128)} %get-tuple-element.15.start_ref, ...), custom_call_target="tpu_custom_call" | custom-call | tf_op jit(solution)/shard_map/pallas_call | solution.py:619

commit v5 on v4

--- a/solution.py
+++ b/solution.py
@@ -71,7 +71,7 @@
     v_in,
     d_in,
     start_ref,
-    gate_ref,
+    row_ref,
     home_c_out,
     home_q,
     home_b,
@@ -485,6 +485,14 @@
     for n in range(1, n_tp):
         remote(gg.at[tp], gg.at[tp], send_sem.at[13], recv_sem.at[5], {"tp": lax.rem(tp + n, n_tp)}).start()
 
+    if n_tp > 1:
+        others = gg.at[pl.ds(0, n_tp - 1)]
+        remote(others, others, send_sem.at[13], recv_sem.at[5], sibling).wait()
+    gate_col = 1.0 / (1.0 + jnp.exp(-logit_col))
+    logit_grad = jnp.sum(gg[...], axis=0)[:, 0:1] * gate_col * (1.0 - gate_col)
+    router = jnp.sum(jnp.where(spots, jnp.broadcast_to(logit_grad, (CAP, TOK)), 0.0), axis=0, keepdims=True)
+    row_ref[...] = router
+
     @pl.when(is_worker)
     def _():
         done()
@@ -499,21 +507,13 @@
         came(home_q, recv_sem.at[6])
         came(home_b, recv_sem.at[7])
 
-    if n_tp > 1:
-        others = gg.at[pl.ds(0, n_tp - 1)]
-        remote(others, others, send_sem.at[13], recv_sem.at[5], sibling).wait()
-    gate_ref[...] = jnp.sum(gg[...], axis=0)
     keep_c.wait()
     remote(counted, counted, send_sem.at[0], recv_sem.at[0], sibling).wait_send()
 
 
-def finish(
-    heads, picked_ref, logit_ref, start_ref, gate_ref, home_c, home_q, home_b, gated_ref, dq_ref, dk_ref, dv_ref, router_ref
-):
-    me = lax.axis_index("seq")
+def finish(heads, start_ref, row_ref, home_c, home_q, home_b, gated_ref, dq_ref, dk_ref, dv_ref, router_ref):
     start = start_ref[...]
-    spots, logit_col = find_logits(me, picked_ref[...], logit_ref[...])
-    gate_col = 1.0 / (1.0 + jnp.exp(-logit_col))
+    router_ref[...] = row_ref[...]
     col = iota((CAP, 128), 1)
     j = iota((CAP, 128), 0)
     from_cls = MSG * ((start + j) & 7)
@@ -529,9 +529,6 @@
         res = dot(take_b, home_b[pl.ds(k * WPH, WPH)].reshape(WPH * MSG, HD))
         dk_ref[:, cols] = res[0:64].astype(BF16)
         dv_ref[:, cols] = res[64:128].astype(BF16)
-    gate_grad = gate_ref[...][:, 0:1]
-    logit_grad = gate_grad * gate_col * (1.0 - gate_col)
-    router_ref[...] = jnp.sum(jnp.where(spots, jnp.broadcast_to(logit_grad, (CAP, TOK)), 0.0), axis=0, keepdims=True)
 
 
 def body(picked, owner_perm, router_logit, queries, keys, values, out_grad):
@@ -545,11 +542,11 @@
     dma = pltpu.SemaphoreType.DMA
     picked = picked.reshape(1, CAP)
     router_logit = router_logit.reshape(2, TOK // 2)
-    start, gate_grad, home_c, home_q, home_b = pl.pallas_call(
+    start, router, home_c, home_q, home_b = pl.pallas_call(
         functools.partial(kernel, n_tp, heads),
         out_shape=(
             jax.ShapeDtypeStruct((1, 128), I32),
-            jax.ShapeDtypeStruct((CAP, 128), F32),
+            jax.ShapeDtypeStruct((1, TOK), F32),
             jax.ShapeDtypeStruct((workers, 8, HD), BF16),
             jax.ShapeDtypeStruct((workers, 8, HD), BF16),
             jax.ShapeDtypeStruct((workers, MSG, HD), BF16),
@@ -625,10 +622,10 @@
             jax.ShapeDtypeStruct((CAP, width), BF16),
             jax.ShapeDtypeStruct((1, TOK), F32),
         ),
-        in_specs=[vmem] * 7,
+        in_specs=[vmem] * 5,
         out_specs=[vmem] * 5,
         compiler_params=pltpu.CompilerParams(vmem_limit_bytes=60 * 1024 * 1024),
-    )(picked, router_logit, start, gate_grad, home_c, home_q, home_b)
+    )(start, router, home_c, home_q, home_b)
     return gated, dq, dk, dv, router.reshape(TOK)
 
 

time: 62.5 us -> 62.6 us (level)
  no operation moved by 1% of the time
where the time goes in v5:
time: 62.6 us; the launch traced here: 62.5 us
  Pallas kernels  61.9 us (99%)
  between operations  0.64 us (1%)
    pallas_call x1, Pallas kernels, body(): pl.pallas_call(functools.partial(kernel, n_tp, heads), out_shape=(jax.Sha...  59.9 us
    pallas_call x1, Pallas kernels, body(): pl.pallas_call(functools.partial(finish, heads), out_shape=(jax.ShapeDtyp...  2 us

profile of v5, /device:TPU:1, one launch (start us, length us, event | category | flops | bytes accessed | tf_op | source)
XLA Modules:
  0.0 62.5 jit_solution(664531637144091256)
XLA Ops:
  0.6 59.9 %shard_map.110 = (s32[1,128]{1,0:T(1,128)}, f32[1,256]{1,0:T(1,128)}, bf16[48,8,128]{2,1,0:T(8,128)(2,1)}, bf16[48,8,128]{2,1,0:T(8,128)(2,1)}, bf16[48,16,128]{2,1,0:T(8,128)(2,1)}) custom-call(s32[1,64]{1,0:T(1,128)} %bitcast.4, s32[1,64]{1,0:T(1,128)} %bitcast.5, bf16[2,128]{1,0:T(2,128)(2,1)} %bitcast.6, bf16[64,768]{1,0:T(8,128)(2,1)} %q_in.1, ...), custom_call_target="tpu_custom_call" | custom-call | tf_op jit(solution)/shard_map/pallas_call | solution.py:545
  60.5 2.0 %shard_map.111 = (bf16[32,768]{1,0:T(8,128)(2,1)}, bf16[64,768]{1,0:T(8,128)(2,1)}, bf16[64,768]{1,0:T(8,128)(2,1)}, bf16[64,768]{1,0:T(8,128)(2,1)}, f32[1,256]{1,0:T(1,128)}) custom-call(s32[1,128]{1,0:T(1,128)} %get-tuple-element.15.start_ref, f32[1,256]{1,0:T(1,128)} %get-tuple-element.16.row_ref, bf16[48,8,128]{2,1,0:T(8,128)(2,1)} %get-tuple-element.17.home_c, ...), custom_call_target="tpu_custom_call" | custom-call | tf_op jit(solution)/shard_map/pallas_call | solution.py:616
